TPU v7x, 256 devices: a whole 4x4x8 slice. The times are simulated.
256 devices in a mesh: rep: 16 (over z, y_hi), seq: 16 (over x, y_lo, core).
Axes of the slice: x: 4, y: 4 (y_hi: 2, y_lo: 2; y = y_hi * 2 + y_lo), z: 8, core: 2. Of those that a mesh axis runs over, the one named last changes fastest.
Arguments:
- tokens: bfloat16 [131072, 4096], P(('rep', 'seq')), may hold values from -24 to 24
- w_query: bfloat16 [4096, 256], P('rep'), may hold values from -0.09375 to 0.09375
- w_key: bfloat16 [4096, 256], P('rep'), may hold values from -0.09375 to 0.09375
- w_value: bfloat16 [4096, 256], P('rep'), may hold values from -0.09375 to 0.09375
- cotangent: bfloat16 [131072, 256], P(('rep', 'seq')), may hold values from -6 to 6
Outputs:
- attended: bfloat16 [131072, 256], P(('rep', 'seq'))
- grad_tokens: bfloat16 [131072, 4096], P(('rep', 'seq'))
- grad_query: float32 [4096, 256], P(('rep', 'seq'))
- grad_key: float32 [4096, 256], P(('rep', 'seq'))
- grad_value: float32 [4096, 256], P(('rep', 'seq'))
All inputs are finite; a program needn't handle non-finite values.
Results may differ from a plain program's by a relative error of at most 0.015.
Values may be sent and summed in bfloat16 or wider, within the bound.
A program may use at most 128 MiB of HBM per device.

v0:
```python
import jax
import jax.numpy as jnp
from jax import lax
from jax.sharding import PartitionSpec as P

HEADS = 2
HD = 128
BLOCK = 512
T_DEV = 512


EPS = 1e-06
highest = lax.Precision.HIGHEST


def carried_in(x, axis, combine, identity, reverse):
    peers, place = (lax.axis_size(axis), lax.axis_index(axis))
    everything = lax.all_gather(x.astype(jnp.bfloat16), axis)
    start = jnp.broadcast_to(jnp.asarray(identity, x.dtype), x.shape)

    def hop(k, before):
        at = peers - 1 - k if reverse else k
        reached = at > place if reverse else at < place
        new = combine(before, everything[at].astype(x.dtype))
        return jnp.where(reached, new, before)

    return lax.fori_loop(0, peers, hop, start)


def add_states(first_part, second_part):
    return first_part + second_part


def body(tokens, w_query, w_key, w_value, cotangent):
    tok_rows = tokens.shape[0]
    blocks = tok_rows // BLOCK
    att_width = HEADS * HD
    shape4 = (blocks, BLOCK, HEADS, HD)
    contract = (((1,), (1,)), ((), ()))
    full_query, full_key, full_value = (
        lax.all_gather(w_query, "rep", axis=0, tiled=True),
        lax.all_gather(w_key, "rep", axis=0, tiled=True),
        lax.all_gather(w_value, "rep", axis=0, tiled=True),
    )
    proj_query = jnp.dot(tokens, full_query, preferred_element_type=jnp.float32)
    proj_key = jnp.dot(tokens, full_key, preferred_element_type=jnp.float32)
    proj_value = jnp.dot(tokens, full_value, preferred_element_type=jnp.float32)
    q_blocks = proj_query.astype(jnp.bfloat16).reshape(shape4)
    k_blocks = proj_key.astype(jnp.bfloat16).reshape(shape4)
    v_blocks = proj_value.astype(jnp.bfloat16).reshape(shape4)
    block_states = jnp.einsum(
        "bshd,bshe->bhde", k_blocks, v_blocks, preferred_element_type=jnp.float32
    )
    own_state = jnp.sum(block_states, 0)
    incoming = carried_in(own_state, "seq", add_states, jnp.zeros_like(own_state), False)
    running = jnp.cumsum(block_states, 0)
    prior_state = incoming[None] + jnp.concatenate([jnp.zeros_like(block_states), running[:-1]], 0)
    causal = lax.broadcasted_iota(jnp.int32, (BLOCK, BLOCK), 0) >= lax.broadcasted_iota(
        jnp.int32, (BLOCK, BLOCK), 1
    )
    scores = jnp.where(
        causal,
        jnp.einsum("bthd,bshd->bhts", q_blocks, k_blocks, preferred_element_type=jnp.float32),
        0.0,
    ).astype(jnp.bfloat16)
    att_mix = jnp.einsum("bhts,bshd->bthd", scores, v_blocks, preferred_element_type=jnp.float32)
    att_mix = att_mix + jnp.einsum(
        "bthd,bhde->bthe", q_blocks.astype(jnp.float32), prior_state, precision=highest
    )
    norm_scale = lax.rsqrt(jnp.mean(att_mix * att_mix, -1, keepdims=True) + EPS)
    attended = (att_mix * norm_scale).astype(jnp.bfloat16).reshape(tok_rows, att_width)
    grad_out = cotangent.astype(jnp.float32).reshape(shape4)
    grad_dot = jnp.mean(grad_out * att_mix, -1, keepdims=True)
    grad_mixed = (
        norm_scale * grad_out - norm_scale * norm_scale * norm_scale * att_mix * grad_dot
    ).astype(jnp.bfloat16)
    block_back = jnp.einsum(
        "bthd,bthe->bhde", q_blocks, grad_mixed, preferred_element_type=jnp.float32
    )
    own_back = jnp.sum(block_back, 0)
    from_later = carried_in(own_back, "seq", add_states, jnp.zeros_like(own_back), True)
    behind = jnp.cumsum(block_back[::-1], 0)[::-1]
    later_state = from_later[None] + jnp.concatenate([behind[1:], jnp.zeros_like(block_back)], 0)
    back_scores = jnp.where(
        causal,
        jnp.einsum("bthe,bshe->bhts", grad_mixed, v_blocks, preferred_element_type=jnp.float32),
        0.0,
    ).astype(jnp.bfloat16)
    grad_q = jnp.einsum(
        "bhts,bshd->bthd", back_scores, k_blocks, preferred_element_type=jnp.float32
    )
    grad_q = grad_q + jnp.einsum(
        "bthe,bhde->bthd", grad_mixed.astype(jnp.float32), prior_state, precision=highest
    )
    grad_k = jnp.einsum(
        "bhts,bthd->bshd", back_scores, q_blocks, preferred_element_type=jnp.float32
    )
    grad_k = grad_k + jnp.einsum(
        "bshe,bhde->bshd", v_blocks.astype(jnp.float32), later_state, precision=highest
    )
    grad_v = jnp.einsum("bhts,bthe->bshe", scores, grad_mixed, preferred_element_type=jnp.float32)
    grad_v = grad_v + jnp.einsum(
        "bshd,bhde->bshe", k_blocks.astype(jnp.float32), later_state, precision=highest
    )
    grad_q = grad_q.astype(jnp.bfloat16).reshape(tok_rows, att_width)
    grad_k = grad_k.astype(jnp.bfloat16).reshape(tok_rows, att_width)
    grad_v = grad_v.astype(jnp.bfloat16).reshape(tok_rows, att_width)
    d_tokens = lax.dot_general(grad_q, full_query, contract, preferred_element_type=jnp.float32)
    d_tokens = d_tokens + lax.dot_general(
        grad_k, full_key, contract, preferred_element_type=jnp.float32
    )
    d_tokens = d_tokens + lax.dot_general(
        grad_v, full_value, contract, preferred_element_type=jnp.float32
    )
    grad_tokens = d_tokens.astype(jnp.bfloat16)
    stacked = jnp.concatenate([grad_q, grad_k, grad_v], 1)
    summed = lax.psum_scatter(
        lax.dot_general(
            tokens, stacked, (((0,), (0,)), ((), ())), preferred_element_type=jnp.float32
        ),
        ("rep", "seq"),
        scatter_dimension=0,
        tiled=True,
    )
    summed = summed * (1.0 / T_DEV)
    return (
        attended,
        grad_tokens,
        summed[:, :att_width],
        summed[:, att_width : 2 * att_width],
        summed[:, 2 * att_width :],
    )


def solution(mesh):
    placed = (
        P(("rep", "seq"), None),
        P("rep", None),
        P("rep", None),
        P("rep", None),
        P(("rep", "seq"), None),
    )
    return jax.shard_map(
        body,
        mesh=mesh,
        in_specs=placed,
        out_specs=(
            P(("rep", "seq"), None),
            P(("rep", "seq"), None),
            P(("rep", "seq"), None),
            P(("rep", "seq"), None),
            P(("rep", "seq"), None),
        ),
        check_vma=False,
    )
```

profile of v0, /device:TPU:1, one launch (start us, length us, event | category | flops | bytes accessed | tf_op | source)
XLA Modules:
  0.0 1684.8 jit_solution(18323291368783423398)
XLA Ops:
  9.4 86.9 %all-gather.8.cloned.1.call-done = bf16[4096,256]{1,0:T(8,128)(2,1)} async-done(((bf16[256,256]{1,0:T(8,128)(2,1)}), bf16[4096,256]{1,0:T(8,128)(2,1)}) %all-gather.8.cloned.1.call-update) | async-done | bytes 2097168 | tf_op jit(solution)/shard_map/all_gather | solution.py:43
  96.3 4.2 convolution_convert_fusion.2
  100.5 80.6 %all-gather.12.cloned.1.call-done = bf16[4096,256]{1,0:T(8,128)(2,1)} async-done(((bf16[256,256]{1,0:T(8,128)(2,1)}), bf16[4096,256]{1,0:T(8,128)(2,1)}) %all-gather.12.cloned.1.call-update) | async-done | bytes 2097168 | tf_op jit(solution)/shard_map/all_gather | solution.py:42
  181.2 4.2 convolution_convert_fusion
  186.5 79.5 %all-gather.10.cloned.1.call-done = bf16[4096,256]{1,0:T(8,128)(2,1)} async-done(((bf16[256,256]{1,0:T(8,128)(2,1)}), bf16[4096,256]{1,0:T(8,128)(2,1)}) %all-gather.10.cloned.1.call-update) | async-done | bytes 2097168 | tf_op jit(solution)/shard_map/all_gather | solution.py:41
  266.0 4.2 convolution_convert_fusion.1
  270.7 33.2 %all-gather.14.cloned.1.call-done = bf16[32,128,128]{2,1,0:T(8,128)(2,1)} async-done(((bf16[2,128,128]{2,1,0:T(8,128)(2,1)}), bf16[32,128,128]{2,1,0:T(8,128)(2,1)}) %all-gather.14.cloned.1.call-update) | async-done | bytes 1048592 | tf_op jit(solution)/shard_map/all_gather | solution.py:18
  303.9 14.8 while.30
  304.8 0.9 add_select_fusion.4
  305.8 0.9 add_select_fusion.4
  306.7 0.9 add_select_fusion.4
  307.6 0.9 add_select_fusion.4
  308.5 0.9 add_select_fusion.4
  309.5 0.9 add_select_fusion.4
  310.4 0.9 add_select_fusion.4
  311.3 0.9 add_select_fusion.4
  312.2 0.9 add_select_fusion.4
  313.2 0.9 add_select_fusion.4
  314.1 0.9 add_select_fusion.4
  315.0 0.9 add_select_fusion.4
  316.0 0.9 add_select_fusion.4
  316.9 0.9 add_select_fusion.4
  317.8 0.9 add_select_fusion.4
  322.0 1.5 select_convert_fusion
  323.5 1.2 fusion.1
  324.7 31.9 %all-gather.16.cloned.1.call-done = bf16[32,128,128]{2,1,0:T(8,128)(2,1)} async-done(((bf16[2,128,128]{2,1,0:T(8,128)(2,1)}), bf16[32,128,128]{2,1,0:T(8,128)(2,1)}) %all-gather.16.cloned.1.call-update) | async-done | bytes 1048592 | tf_op jit(solution)/shard_map/all_gather | solution.py:18
  356.6 14.9 while.31
  357.6 0.9 add_select_fusion.5
  358.5 0.9 add_select_fusion.5
  359.4 0.9 add_select_fusion.5
  360.3 0.9 add_select_fusion.5
  361.3 0.9 add_select_fusion.5
  362.2 0.9 add_select_fusion.5
  363.1 0.9 add_select_fusion.5
  364.1 0.9 add_select_fusion.5
  365.0 0.9 add_select_fusion.5
  365.9 0.9 add_select_fusion.5
  366.9 0.9 add_select_fusion.5
  367.8 0.9 add_select_fusion.5
  373.0 1.2 copy-done.10
  374.3 6.3 convolution_bitcast_fusion
  380.6 12.6 copy.56
  393.3 0.9 copy-done.3
  395.0 1.3 fusion.14
  396.6 1.3 fusion.16
  398.2 3.3 add_convert_fusion
  401.5 1273.3 %reduce-scatter.4.cloned.1.call-done = f32[16,768]{1,0:T(8,128)} async-done(((f32[4096,768]{1,0:T(8,128)}), f32[16,768]{1,0:T(8,128)}) %reduce-scatter.4.cloned.1.call-update) | async-done | bytes 49168
  1674.9 1.0 copy.57
  (59 shorter events, 16.7 us)
Async XLA Ops:
  7.2 89.2 %all-gather.8.cloned.1.call-start = ((), (), s32[]{:S(2)}) async-start(), calls=%async_computation.1 | async-start | bytes 2228224 | tf_op jit(solution)/shard_map/all_gather | solution.py:43
  7.9 173.3 %all-gather.12.cloned.1.call-start = ((), (), s32[]{:S(2)}) async-start(), calls=%async_computation.3 | async-start | bytes 2228224 | tf_op jit(solution)/shard_map/all_gather | solution.py:42
  8.6 257.3 %all-gather.10.cloned.1.call-start = ((), (), s32[]{:S(2)}) async-start(), calls=%async_computation.2 | async-start | bytes 2228224 | tf_op jit(solution)/shard_map/all_gather | solution.py:41
  9.4 294.5 %all-gather.14.cloned.1.call-start = ((), (), s32[]{:S(2)}) async-start(), calls=%async_computation.4 | async-start | bytes 1114112 | tf_op jit(solution)/shard_map/all_gather | solution.py:18
  100.5 85.8 %copy-start.8 = (bf16[512,256]{1,0:T(8,128)(2,1)S(1)}, bf16[512,256]{1,0:T(8,128)(2,1)}, u32[]{:S(2)}) copy-start(bf16[512,256]{1,0:T(8,128)(2,1)} %param.13) | copy-start | bytes 786436
  186.2 170.4 %all-gather.16.cloned.1.call-start = ((), (), s32[]{:S(2)}) async-start(), calls=%async_computation.5 | async-start | bytes 1114112 | tf_op jit(solution)/shard_map/all_gather | solution.py:18
  186.5 83.6 %copy-start.9 = (pred[512,512]{1,0:T(8,128)(4,1)}, pred[512,512]{1,0:T(8,128)(4,1)S(1)}, u32[]{:S(2)}) copy-start(pred[512,512]{1,0:T(8,128)(4,1)S(1)} %iota_compare_fusion) | copy-start | bytes 786436
  321.4 1353.5 %reduce-scatter.4.cloned.1.call-start = ((), (), s32[]{:S(2)}) async-start(), calls=%async_computation.6 | async-start | bytes 12632064
  371.9 2.3 copy-start.10
  372.3 2.0 copy-start.4
  372.9 7.7 copy-start.6
  393.2 0.9 copy-start.3
  393.2 1.8 copy-start.2
  393.2 1.8 copy-start.5
  395.0 1.6 copy-start.1
  395.0 1.6 copy-start.7
  396.6 1.6 copy-start
Sparse Core Ops, SparseCore 0:
  10.6 85.7 all-gather.7
  98.9 82.1 all-gather.11
  183.8 82.1 all-gather.9
  268.3 35.6 all-gather.13
  321.5 35.0 all-gather.15
  393.4 1281.4 reduce-scatter.3
where the time goes:
time: 1690 us; the launch traced here: 1680 us
  waiting for transfers between devices  1590 us (94%)
  matrix products  32.4 us (2%)
  other arithmetic  29.9 us (2%)
  local copies, waits for them, and re-layouts  19.4 us (1%)
    unnamed x7, waiting for transfers between devices  1280 us
    all_gather x1, waiting for transfers between devices, body(): lax.all_gather(w_value, 'rep', axis=0, tiled=True)  86.9 us
    all_gather x1, waiting for transfers between devices, body(): lax.all_gather(w_key, 'rep', axis=0, tiled=True)  80.6 us
    all_gather x1, waiting for transfers between devices, body(): lax.all_gather(w_query, 'rep', axis=0, tiled=True)  79.5 us
    all_gather x2, waiting for transfers between devices, carried_in(): everything = lax.all_gather(x.astype(jnp.bfloat16), axis)  65.1 us
  transfers between devices with their start and end apart: 6, of which 6 were waited for; matrix products, arithmetic and copies ran while one was open for 1% of the time, Pallas kernels for 0%

commit v1 on v0

v1 whole, which is shorter than its diff:
```python
import jax
import jax.numpy as jnp
from jax import lax
from jax.experimental import pallas as pl
from jax.experimental.pallas import tpu as pltpu
from jax.sharding import PartitionSpec as P

D = 4096
HD = 128
T_DEV = 512
EPS = 1e-06
MESH = pl.DeviceIdType.MESH
f32 = jnp.float32
bf16 = jnp.bfloat16
N_SEM = 160
BLK = (8, 2, 4, 2, 32, 128)


def mod(a, n):
    return lax.rem(a, jnp.int32(n))


def dot(a, b, ca=1, cb=0):
    return lax.dot_general(a, b, (((ca,), (cb,)), ((), ())), preferred_element_type=f32)


def split(a):
    hi = a.astype(bf16)
    return hi, (a - hi.astype(f32)).astype(bf16)


class Net:
    def __init__(self, send_sems, recv_sems):
        self.ss, self.rs, self.n, self.open = send_sems, recv_sems, 0, []

    def make(self, src, dst, to):
        i = self.n
        self.n += 1
        assert i < N_SEM
        return pltpu.make_async_remote_copy(
            src_ref=src, dst_ref=dst, send_sem=self.ss.at[i], recv_sem=self.rs.at[i], device_id=to, device_id_type=MESH
        )

    def send(self, src, dst, to):
        cp = self.make(src, dst, to)
        cp.start()
        self.open.append((cp, None))
        return cp

    def send_if(self, cond, src, dst, to):
        cp = self.make(src, dst, to)
        pl.when(cond)(cp.start)
        self.open.append((cp, cond))
        return cp

    def finish(self):
        for cp, cond in self.open:
            if cond is None:
                cp.wait_send()
            else:
                pl.when(cond)(cp.wait_send)


def kernel(
    tok_hbm, wq, wk, wv, cot, att_o, gt_hbm, gq_o, gk_o, gv_o,
    tok, w0, w1, w2, o0, o1, o2, qkv, cotb, scores, mixl, dmix, d_all, d_oth, att_oth, att_snd,
    st_snd, st_rcv, bk_snd, bk_rcv, prior, later,
    p0, p1, p2, sa, ra, sb, rb, sc, rc, acc_a, acc_b, acc_c,
    sa_y, ra_y, sa_x, ra_x, acc_a2, sb_y, rb_y, sb_z, rb_z, acc_b2, sc_x, rc_x, sc_z, rc_z, acc_c2,
    fin, fin_oth, gt_buf, send_sems, recv_sems, loc_sems,
):
    rep, seq = lax.axis_index("rep"), lax.axis_index("seq")
    z, yh = lax.div(rep, jnp.int32(2)), mod(rep, 2)
    x, yl, c = lax.div(seq, jnp.int32(4)), mod(lax.div(seq, jnp.int32(2)), 2), mod(seq, 2)
    y = yh * 2 + yl
    oc = 1 - c

    def dev(x_, y_, z_, c_):
        return {"rep": z_ * 2 + lax.div(y_, jnp.int32(2)), "seq": x_ * 4 + mod(y_, 2) * 2 + c_}

    def xd(k):
        return dev(mod(x + k, 4), y, z, c)

    def yd(k):
        return dev(x, mod(y + k, 4), z, c)

    def zd(k):
        return dev(x, y, mod(z + k, 8), c)

    partner = dev(x, y, z, oc)
    across = dev(x, 3 - y, z, c)
    group = [(dx, dl) for dx in range(4) for dl in range(2) if dx or dl]

    def gd(dx, dl):
        return dev(mod(x + dx, 4), yh * 2 + mod(yl + dl, 2), z, c)

    def place(dx, dl):
        return mod(x + dx, 4) * 2 + mod(yl + dl, 2)

    here = x * 2 + yl

    tok_cp = pltpu.make_async_copy(tok_hbm, tok.at[pl.ds(pl.multiple_of(c * 512, 512), 512)], loc_sems.at[0])
    tok_cp.start()
    peers = [partner] + [xd(k) for k in (1, 2, 3)] + [yd(k) for k in (1, 2, 3)] + [zd(k) for k in range(1, 8)]
    peers += [gd(dx, 1) for dx in (1, 2, 3)]
    bar = pltpu.get_barrier_semaphore()
    lane_c = pl.ds(pl.multiple_of(c * HD, HD), HD)
    lane_o = pl.ds(pl.multiple_of(oc * HD, HD), HD)
    for w, src in ((w0, wq), (w1, wk), (w2, wv)):
        w[z, yh] = src[:, lane_c].reshape(BLK[2:])
    for to in peers:
        pl.semaphore_signal(bar, inc=1, device_id=to, device_id_type=MESH)
    cotb[c] = cot[:, lane_c]
    pl.semaphore_wait(bar, len(peers))

    net = Net(send_sems, recv_sems)

    b_z = [net.send(w1.at[z, yh, x, yl], w1.at[z, yh, x, yl], zd(k)) for k in (1, 7, 2, 6, 3, 5, 4)]
    c_z = [net.send(w2.at[z, yh, x, yl], w2.at[z, yh, x, yl], zd(k)) for k in (1, 7, 2, 6, 3, 5, 4)]
    a_y = net.send(w0.at[z, yh], w0.at[z, yh], across)
    oyh = 1 - yh

    def a_send(at, half, k):
        return net.send(w0.at[at, half], w0.at[at, half], zd(k))

    a1 = [a_send(z, yh, 1), a_send(z, yh, 7)]
    cot_cp = net.send(cot.at[:, lane_o], cotb.at[c], partner)
    tok_x = net.send(tok_hbm, tok.at[pl.ds(pl.multiple_of(c * 512, 512), 512)], partner)
    a_y.wait_recv()
    a1 += [a_send(z, oyh, 1), a_send(z, oyh, 7)]
    for cp in b_z:
        cp.wait_recv()
    all_z = pl.ds(0, 8)
    b_y = [net.send(w1.at[all_z, yh, x, yl], w1.at[all_z, yh, x, yl], yd(k)) for k in (1, 3, 2)]
    for cp in c_z:
        cp.wait_recv()
    c_x = [net.send(w2.at[all_z, yh, x, yl], w2.at[all_z, yh, x, yl], xd(k)) for k in (1, 3, 2)]

    def a_step(prev, k):
        out = []
        for i, half in ((0, yh), (2, oyh)):
            prev[i].wait_recv()
            out.append(a_send(mod(z + 8 - k, 8), half, 1))
            prev[i + 1].wait_recv()
            out.append(a_send(mod(z + k, 8), half, 7))
        return out

    a2 = a_step(a1, 1)
    lo, hi = pl.ds(0, 4), pl.ds(4, 4)
    for cp in b_y:
        cp.wait_recv()
    b_x = []
    for first, second in ((lo, hi),):
        b_x.append(net.send(w1.at[first, :, x], w1.at[first, :, x], xd(1)))
        b_x.append(net.send(w1.at[second, :, x], w1.at[second, :, x], xd(3)))
        b_x.append(net.send(w1.at[second, :, x], w1.at[second, :, x], xd(1)))
        b_x.append(net.send(w1.at[first, :, x], w1.at[first, :, x], xd(3)))
    for cp in c_x:
        cp.wait_recv()
    c_y = [
        net.send(w2.at[lo, yh, :, yl], w2.at[lo, yh, :, yl], yd(1)),
        net.send(w2.at[hi, yh, :, yl], w2.at[hi, yh, :, yl], yd(3)),
        net.send(w2.at[hi, yh, :, yl], w2.at[hi, yh, :, yl], yd(1)),
        net.send(w2.at[lo, yh, :, yl], w2.at[lo, yh, :, yl], yd(3)),
    ]
    a3 = a_step(a2, 2)
    b_x[0].wait_recv()
    xm, xp = mod(x + 3, 4), mod(x + 1, 4)
    b_f = [net.send(w1.at[lo, :, xm], w1.at[lo, :, xm], xd(1))]
    b_x[1].wait_recv()
    b_f += [net.send(w1.at[hi, :, xp], w1.at[hi, :, xp], xd(3))]
    ym, yp = mod(y + 3, 4), mod(y + 1, 4)
    ymh, yml, yph, ypl = lax.div(ym, jnp.int32(2)), mod(ym, 2), lax.div(yp, jnp.int32(2)), mod(yp, 2)
    c_y[0].wait_recv()
    c_f = [net.send(w2.at[lo, ymh, :, yml], w2.at[lo, ymh, :, yml], yd(1))]
    c_y[1].wait_recv()
    c_f += [net.send(w2.at[hi, yph, :, ypl], w2.at[hi, yph, :, ypl], yd(3))]
    for cp in a3:
        cp.wait_recv()
    a4 = [a_send(mod(z + 5, 8), 0, 1), a_send(mod(z + 3, 8), 1, 7)]
    tok_cp.wait()
    tok_x.wait_recv()
    cot_cp.wait_recv()
    for cp in b_x[2:] + b_f:
        cp.wait_recv()
    w1_x = net.send(w1, o1, partner)
    for cp in c_y[2:] + c_f:
        cp.wait_recv()
    w2_x = net.send(w2, o2, partner)

    @pl.loop(0, 4)
    def _(i):
        r = pl.ds(pl.multiple_of(i * 256, 256), 256)
        w = jnp.concatenate([w1[...].reshape(D, HD), w2[...].reshape(D, HD)], 1)
        qkv[r, 128:384] = dot(tok[r, :], w).astype(bf16)

    rows = [slice(0, 512), slice(512, 1024)]
    state = [dot(qkv[r, 128:256], qkv[r, 256:384], 0, 0) for r in rows]
    st_snd[...] = (state[0] + state[1]).astype(bf16)
    prior[0] = jnp.zeros((HD, HD), f32)
    prior[1] = state[0]
    st = [net.send_if(place(dx, dl) > here, st_snd, st_rcv.at[i], gd(dx, dl)) for i, (dx, dl) in enumerate(group)]

    for cp in a4:
        cp.wait_recv()
    w0_x = net.send(w0, o0, partner)

    @pl.loop(0, 4)
    def _(i):
        r = pl.ds(pl.multiple_of(i * 256, 256), 256)
        qkv[r, 0:128] = dot(tok[r, :], w0[...].reshape(D, HD)).astype(bf16)

    causal = lax.broadcasted_iota(jnp.int32, (512, 512), 0) >= lax.broadcasted_iota(jnp.int32, (512, 512), 1)
    for b, r in enumerate(rows):
        scores[b] = jnp.where(causal, dot(qkv[r, 0:128], qkv[r, 128:256], 1, 1), 0.0).astype(bf16)
        mixl[b] = dot(scores[b], qkv[r, 256:384])
    for i, (dx, dl) in enumerate(group):

        @pl.when(place(4 - dx, dl) < here)
        def _(i=i):
            st[i].wait_recv()
            got = st_rcv[i].astype(f32)
            prior[0] += got
            prior[1] += got

    back = []
    for b, r in enumerate(rows):
        p_hi, p_lo = split(prior[b])
        q = qkv[r, 0:128]
        mix = mixl[b] + (dot(q, p_hi) + dot(q, p_lo))
        s = lax.rsqrt(jnp.mean(mix * mix, -1, keepdims=True) + EPS)
        att_snd[b] = (mix * s).astype(bf16)
        g = cotb[b].astype(f32)
        m = jnp.mean(g * mix, -1, keepdims=True)
        dmix[b] = (s * g - s * s * s * mix * m).astype(bf16)
        back.append(dot(q, dmix[b], 0, 0))
    bk_snd[...] = (back[0] + back[1]).astype(bf16)
    later[1] = jnp.zeros((HD, HD), f32)
    later[0] = back[1]
    bk = [net.send_if(place(dx, dl) < here, bk_snd, bk_rcv.at[i], gd(dx, dl)) for i, (dx, dl) in enumerate(group)]
    att_x = net.send(att_snd.at[oc], att_oth, partner)
    att_o[:, lane_c] = att_snd[c]

    d_loc = []
    for b, r in enumerate(rows):
        q, k, v = qkv[r, 0:128], qkv[r, 128:256], qkv[r, 256:384]
        bs = jnp.where(causal, dot(dmix[b], v, 1, 1), 0.0).astype(bf16)
        p_hi, p_lo = split(prior[b])
        d_all[r, 0:128] = (dot(bs, k) + (dot(dmix[b], p_hi, 1, 1) + dot(dmix[b], p_lo, 1, 1))).astype(bf16)
        mixl[b] = dot(bs, q, 0, 0)
        d_loc.append(dot(scores[b], dmix[b], 0, 0))

    def p_q(k):
        at = mod(z + k, 8)
        cols = pl.ds(pl.multiple_of(at * 512, 512), 512)
        p0[at] = dot(tok[:, cols], d_all[:, 0:128], 0, 0).reshape(BLK[1:])

    def a_out(way, step, half, plus):
        k = 5 - step
        at = mod(z + (k if way == 0 else 8 - k), 8)
        val = p0[at, half]
        if plus is not None:
            plus.wait_recv()
            val = val + ra[way, step - 2, half].astype(f32)
        sa[way, step - 1, half] = val.astype(bf16)
        return net.send(sa.at[way, step - 1, half], ra.at[way, step - 1, half], zd(1 if way == 0 else 7))

    p_q(4)
    r1 = [a_out(0, 1, 0, None), a_out(1, 1, 1, None)]
    p_q(3)
    r2r = [None, a_out(0, 2, 1, None)]
    p_q(5)
    r2l = [a_out(1, 2, 0, None), None]
    r2r[0] = a_out(0, 2, 0, r1[0])
    r2l[1] = a_out(1, 2, 1, r1[1])
    p_q(2)
    p_q(6)
    r3r = [None, a_out(0, 3, 1, r2r[1])]
    r3l = [a_out(1, 3, 0, r2l[0]), None]
    p_q(1)
    p_q(7)
    p_q(0)

    for i, (dx, dl) in enumerate(group):

        @pl.when(place(4 - dx, dl) > here)
        def _(i=i):
            bk[i].wait_recv()
            got = bk_rcv[i].astype(f32)
            later[0] += got
            later[1] += got

    for b, r in enumerate(rows):
        l_hi, l_lo = split(later[b])
        k, v = qkv[r, 128:256], qkv[r, 256:384]
        d_all[r, 128:256] = (mixl[b] + (dot(v, l_hi, 1, 1) + dot(v, l_lo, 1, 1))).astype(bf16)
        d_all[r, 256:384] = (d_loc[b] + (dot(k, l_hi) + dot(k, l_lo))).astype(bf16)
    d_x = net.send(d_all.at[pl.ds(pl.multiple_of(oc * 512, 512), 512)], d_oth, partner)

    r3r[0] = a_out(0, 3, 0, r2r[0])
    r3l[1] = a_out(1, 3, 1, r2l[1])

    def p_kv(first):
        @pl.loop(first, first + 4)
        def _(j):
            cols = pl.ds(pl.multiple_of(j * 512, 512), 512)
            got = dot(tok[:, cols], d_all[:, 128:384], 0, 0)
            p1[j] = got[:, 0:128].reshape(BLK[1:])
            p2[j] = got[:, 128:256].reshape(BLK[1:])

    def halves(h):
        return pl.ds(4 * h, 4)

    def b_out(way, step, h, plus):
        k = 3 - step
        at = mod(x + (k if way == 0 else 4 - k), 4)
        val = p1[halves(h), :, at]
        if plus is not None:
            plus.wait_recv()
            val = val + rb[way, 0, halves(h)].astype(f32)
        sb[way, step - 1, halves(h)] = val.astype(bf16)
        return net.send(sb.at[way, step - 1, halves(h)], rb.at[way, step - 1, halves(h)], xd(1 if way == 0 else 3))

    def c_out(way, step, h, plus):
        k = 3 - step
        at = mod(y + (k if way == 0 else 4 - k), 4)
        ah, al = lax.div(at, jnp.int32(2)), mod(at, 2)
        val = p2[halves(h), ah, :, al]
        if plus is not None:
            plus.wait_recv()
            val = val + rc[way, 0, halves(h)].astype(f32)
        sc[way, step - 1, halves(h)] = val.astype(bf16)
        return net.send(sc.at[way, step - 1, halves(h)], rc.at[way, step - 1, halves(h)], yd(1 if way == 0 else 3))

    p_kv(0)
    b1r, c1r = b_out(0, 1, 0, None), c_out(0, 1, 0, None)
    b2l, c2l = [b_out(1, 2, 0, None)], [c_out(1, 2, 0, None)]
    r4 = [a_out(0, 4, 1, r3r[1]), a_out(1, 4, 0, r3l[0])]
    p_kv(4)
    b1l, c1l = b_out(1, 1, 1, None), c_out(1, 1, 1, None)
    b2r, c2r = [b_out(0, 2, 1, None)], [c_out(0, 2, 1, None)]
    r4 += [a_out(0, 4, 0, r3r[0]), a_out(1, 4, 1, r3l[1])]

    d_x.wait_recv()
    for cp in (w0_x, w1_x, w2_x):
        cp.wait_recv()
    mine = pl.ds(pl.multiple_of(c * 512, 512), 512)

    def g_t(first, last):
        @pl.loop(first, last)
        def _(j):
            w = jnp.concatenate([ref[j].reshape(512, HD) for ref in (w0, w1, w2, o0, o1, o2)], 1)
            d = jnp.concatenate([d_all[mine, :], d_oth[...]], 1)
            cols = pl.ds(pl.multiple_of(j * 512, 512), 512)
            gt_buf[:, cols] = dot(d, w, 1, 1).astype(bf16)
            pltpu.make_async_copy(gt_buf.at[:, cols], gt_hbm.at[:, cols], loc_sems.at[1 + j]).start()

    g_t(0, 2)
    b2r.append(b_out(0, 2, 0, b1r))
    c2r.append(c_out(0, 2, 0, c1r))
    b2l.append(b_out(1, 2, 1, b1l))
    c2l.append(c_out(1, 2, 1, c1l))
    g_t(2, 5)
    for cp in r4:
        cp.wait_recv()
    acc_a[...] = p0[z] + ra[0, 3].astype(f32) + ra[1, 3].astype(f32)
    a_y2 = []
    for k in (1, 2, 3):
        at = mod(y + k, 4)
        sa_y[k - 1] = acc_a[lax.div(at, jnp.int32(2)), :, mod(at, 2)].astype(bf16)
        a_y2.append(net.send(sa_y.at[k - 1], ra_y.at[k - 1], yd(k)))
    g_t(5, 8)
    for cp in b2r + b2l:
        cp.wait_recv()
    acc_b[...] = p1[:, :, x] + rb[0, 1].astype(f32) + rb[1, 1].astype(f32)
    b_y2 = []
    for k in (1, 2, 3):
        at = mod(y + k, 4)
        sb_y[k - 1] = acc_b[:, lax.div(at, jnp.int32(2)), mod(at, 2)].astype(bf16)
        b_y2.append(net.send(sb_y.at[k - 1], rb_y.at[k - 1], yd(k)))
    for cp in c2r + c2l:
        cp.wait_recv()
    acc_c[...] = p2[:, yh, :, yl] + rc[0, 1].astype(f32) + rc[1, 1].astype(f32)
    c_x2 = []
    for k in (1, 2, 3):
        sc_x[k - 1] = acc_c[:, mod(x + k, 4)].astype(bf16)
        c_x2.append(net.send(sc_x.at[k - 1], rc_x.at[k - 1], xd(k)))
    for cp in a_y2:
        cp.wait_recv()
    acc_a2[...] = acc_a[yh, :, yl] + sum(ra_y[k].astype(f32) for k in range(3))
    a_x2 = []
    for k in (1, 2, 3):
        sa_x[k - 1] = acc_a2[mod(x + k, 4)].astype(bf16)
        a_x2.append(net.send(sa_x.at[k - 1], ra_x.at[k - 1], xd(k)))
    for cp in b_y2:
        cp.wait_recv()
    acc_b2[...] = acc_b[:, yh, yl] + sum(rb_y[k].astype(f32) for k in range(3))
    b_z2 = []
    for k in range(1, 8):
        sb_z[k - 1] = acc_b2[mod(z + k, 8)].astype(bf16)
        b_z2.append(net.send(sb_z.at[k - 1], rb_z.at[k - 1], zd(k)))
    for cp in c_x2:
        cp.wait_recv()
    acc_c2[...] = acc_c[:, x] + sum(rc_x[k].astype(f32) for k in range(3))
    c_z2 = []
    for k in range(1, 8):
        sc_z[k - 1] = acc_c2[mod(z + k, 8)].astype(bf16)
        c_z2.append(net.send(sc_z.at[k - 1], rc_z.at[k - 1], zd(k)))
    for cp in a_x2:
        cp.wait_recv()
    scale = 1.0 / T_DEV
    fin[0] = ((acc_a2[x] + sum(ra_x[k].astype(f32) for k in range(3))) * scale).reshape(2, 16, HD)
    for cp in b_z2:
        cp.wait_recv()
    fin[1] = ((acc_b2[z] + sum(rb_z[k].astype(f32) for k in range(7))) * scale).reshape(2, 16, HD)
    for cp in c_z2:
        cp.wait_recv()
    fin[2] = ((acc_c2[z] + sum(rc_z[k].astype(f32) for k in range(7))) * scale).reshape(2, 16, HD)
    fin_x = net.send(fin.at[:, oc], fin_oth, partner)
    for i, o in enumerate((gq_o, gk_o, gv_o)):
        o[:, lane_c] = fin[i, c]
    att_x.wait_recv()
    att_o[:, lane_o] = att_oth[...]

    @pl.loop(0, 8)
    def _(j):
        cols = pl.ds(pl.multiple_of(j * 512, 512), 512)
        pltpu.make_async_copy(gt_buf.at[:, cols], gt_hbm.at[:, cols], loc_sems.at[1 + j]).wait()

    fin_x.wait_recv()
    for i, o in enumerate((gq_o, gk_o, gv_o)):
        o[:, lane_o] = fin_oth[i]
    net.finish()


def body(tokens, w_query, w_key, w_value, cotangent):
    vm, any_ = pl.BlockSpec(memory_space=pltpu.VMEM), pl.BlockSpec(memory_space=pl.ANY)

    def v(*shape, t=bf16):
        return pltpu.VMEM(shape, t)

    scratch = [v(1024, D)] + [v(*BLK)] * 6
    scratch += [v(1024, 384), v(2, 512, 128), v(2, 512, 512), v(2, 512, 128, t=f32), v(2, 512, 128)]
    scratch += [v(1024, 384), v(512, 384), v(512, 128), v(2, 512, 128)]
    scratch += [v(128, 128), v(7, 128, 128), v(128, 128), v(7, 128, 128), v(2, 128, 128, t=f32), v(2, 128, 128, t=f32)]
    scratch += [v(*BLK, t=f32)] * 3
    scratch += [v(2, 4, 2, 4, 2, 32, 128)] * 2 + [v(2, 2, 8, 2, 2, 32, 128)] * 2 + [v(2, 2, 8, 4, 32, 128)] * 2
    scratch += [v(2, 4, 2, 32, 128, t=f32), v(8, 2, 2, 32, 128, t=f32), v(8, 4, 32, 128, t=f32)]
    scratch += [v(3, 4, 32, 128)] * 2 + [v(3, 32, 128)] * 2 + [v(4, 32, 128, t=f32)]
    scratch += [v(3, 8, 32, 128)] * 2 + [v(7, 32, 128)] * 2 + [v(8, 32, 128, t=f32)]
    scratch += [v(3, 8, 32, 128)] * 2 + [v(7, 32, 128)] * 2 + [v(8, 32, 128, t=f32)]
    scratch += [v(3, 2, 16, 128, t=f32), v(3, 16, 128, t=f32), v(512, D)]
    scratch += [pltpu.SemaphoreType.DMA((N_SEM,)), pltpu.SemaphoreType.DMA((N_SEM,)), pltpu.SemaphoreType.DMA((9,))]
    grad = jax.ShapeDtypeStruct((16, 256), f32)
    return pl.pallas_call(
        kernel,
        out_shape=(
            jax.ShapeDtypeStruct((T_DEV, 256), bf16),
            jax.ShapeDtypeStruct((T_DEV, D), bf16),
            grad,
            grad,
            grad,
        ),
        in_specs=[any_, vm, vm, vm, vm],
        out_specs=(vm, any_, vm, vm, vm),
        scratch_shapes=scratch,
        compiler_params=pltpu.CompilerParams(collective_id=0, has_side_effects=True, vmem_limit_bytes=60 * 2**20),
        cost_estimate=pl.CostEstimate(flops=10**10, bytes_accessed=10**7, transcendentals=1024),
        name="step",
    )(tokens, w_query, w_key, w_value, cotangent)


def solution(mesh):
    both = P(("rep", "seq"), None)
    rep = P("rep", None)
    return jax.shard_map(
        body, mesh=mesh, in_specs=(both, rep, rep, rep, both), out_specs=(both,) * 5, check_vma=False
    )
```

time: 1690 us -> 90 us (0.05)
  waiting for transfers between devices: 1590 us -> 0 us
  Pallas kernels: 0 us -> 81 us
  matrix products: 32.4 us -> 0 us
  other arithmetic: 29.9 us -> 0 us
    unnamed x7 -> x0, waiting for transfers between devices: 1280 us -> none
    all_gather x5 -> x0, waiting for transfers between devices: 312 us -> none  [the longest x1 86.9 us: body(): lax.all_gather(w_value, 'rep', axis=0, tiled=True)]
    pallas_call x0 -> x1, Pallas kernels: none -> 81 us  [body(): pl.pallas_call(kernel, out_shape=(jax.ShapeDtypeStruct((T_DEV, 256), bf16...]
    dot_general x19 -> x0, matrix products: 32.4 us -> none  [the longest x1 6.34 us: body(): lax.dot_general(tokens, stacked, (((0,), (0,)), ((), ())), preferred_elem...]
    select_n x32 -> x0, other arithmetic: 28.9 us -> none  [hop(): return jnp.where(reached, new, before)]
  transfers between devices with their start and end apart: 6 -> 0, of which waited for: 6 -> 0; matrix products, arithmetic and copies ran while one was open for 1% -> 0% of each run, Pallas kernels for 0% -> 0%
where the time goes in v1:
time: 90 us; the launch traced here: 89.8 us
  Pallas kernels  81 us (90%)
  local copies, waits for them, and re-layouts  8.22 us (9%)
    pallas_call x1, Pallas kernels, body(): pl.pallas_call(kernel, out_shape=(jax.ShapeDtypeStruct((T_DEV, 256), bf16...  81 us
    unnamed x11, local copies, waits for them, and re-layouts  8.22 us

profile of v1, /device:TPU:1, one launch (start us, length us, event | category | flops | bytes accessed | tf_op | source)
XLA Modules:
  0.0 89.8 jit_solution(8087875187042572139)
XLA Ops:
  0.6 81.0 %step.1 = (bf16[512,256]{1,0:T(8,128)(2,1)}, bf16[512,4096]{1,0:T(8,128)(2,1)}, f32[16,256]{1,0:T(8,128)}, f32[16,256]{1,0:T(8,128)}, f32[16,256]{1,0:T(8,128)}) custom-call(bf16[512,4096]{1,0:T(8,128)(2,1)} %tok_hbm.1, bf16[256,256]{1,0:T(8,128)(2,1)} %wq.1, bf16[256,256]{1,0:T(8,128)(2,1)} %wk.1, bf16[256,256]{1,0:T(8,128)(2,1)} %wv.1, bf16[512,256]{1,0:T(8,128)(2,1)} %cot.1), custom_call_target="tpu_custom_call" | custom-call | flops 10000000000 | bytes 10000000 | tf_op jit(solution)/shard_map/step/pallas_call | solution.py:455
  81.6 1.7 %copy.15 = bf16[512,256]{1,0:T(8,128)(2,1)} copy(bf16[512,256]{1,0:T(8,128)(2,1)} %get-tuple-element.10) | data formatting | bytes 524288
  83.3 0.0 copy-start.2
  83.3 0.0 copy-start.1
  83.3 0.0 copy-start
  83.3 4.7 %copy.16 = bf16[512,4096]{1,0:T(8,128)(2,1)} copy(bf16[512,4096]{1,0:T(8,128)(2,1)} %get-tuple-element.11) | data formatting | bytes 8388608
  88.0 0.0 copy-done.2
  88.0 0.6 copy.17
  88.6 0.0 copy-done.1
  88.6 0.6 copy.18
  89.2 0.0 copy-done
  89.2 0.6 copy.19
Async XLA Ops:
  83.3 4.7 %copy-start.2 = (f32[16,256]{1,0:T(8,128)S(1)}, f32[16,256]{1,0:T(8,128)}, u32[]{:S(2)}) copy-start(f32[16,256]{1,0:T(8,128)} %get-tuple-element.12) | copy-start | bytes 49156
  83.3 5.3 %copy-start.1 = (f32[16,256]{1,0:T(8,128)S(1)}, f32[16,256]{1,0:T(8,128)}, u32[]{:S(2)}) copy-start(f32[16,256]{1,0:T(8,128)} %get-tuple-element.13) | copy-start | bytes 49156
  83.3 5.9 %copy-start = (f32[16,256]{1,0:T(8,128)S(1)}, f32[16,256]{1,0:T(8,128)}, u32[]{:S(2)}) copy-start(f32[16,256]{1,0:T(8,128)} %get-tuple-element.14) | copy-start | bytes 49156

commit v2 on v1

v2 whole, which is shorter than its diff:
```python
import jax
import jax.numpy as jnp
from jax import lax
from jax.experimental import pallas as pl
from jax.experimental.pallas import tpu as pltpu
from jax.sharding import PartitionSpec as P

D = 4096
HD = 128
T_DEV = 512
EPS = 1e-06
MESH = pl.DeviceIdType.MESH
f32 = jnp.float32
bf16 = jnp.bfloat16
N_SEM = 256
BLK = (8, 2, 4, 2, 32, 128)


def mod(a, n):
    return lax.rem(a, jnp.int32(n))


def dot(a, b, ca=1, cb=0):
    return lax.dot_general(a, b, (((ca,), (cb,)), ((), ())), preferred_element_type=f32)


def split(a):
    hi = a.astype(bf16)
    return hi, (a - hi.astype(f32)).astype(bf16)


class Net:
    def __init__(self, send_sems, recv_sems):
        self.ss, self.rs, self.n, self.open = send_sems, recv_sems, 0, []

    def make(self, src, dst, to):
        i = self.n
        self.n += 1
        assert i < N_SEM
        return pltpu.make_async_remote_copy(
            src_ref=src, dst_ref=dst, send_sem=self.ss.at[i], recv_sem=self.rs.at[i], device_id=to, device_id_type=MESH
        )

    def send(self, src, dst, to):
        cp = self.make(src, dst, to)
        cp.start()
        self.open.append((cp, None))
        return cp

    def send_if(self, cond, src, dst, to):
        cp = self.make(src, dst, to)
        pl.when(cond)(cp.start)
        self.open.append((cp, cond))
        return cp

    def finish(self):
        for cp, cond in self.open:
            if cond is None:
                cp.wait_send()
            else:
                pl.when(cond)(cp.wait_send)


OFF = (0, 1, 7, 2, 6, 3, 5, 4)
SLOT = {k: p for p, k in enumerate(OFF)}
GROUPS = ((0, 1), (1, 3), (3, 5), (5, 8))


def back(k):
    return (8 - k) % 8


def kernel(
    tok_hbm, wq, wk, wv, cot, att_o, gt_o, gq_o, gk_o, gv_o,
    tok, w0, w1, w2, o0, o1, o2, acc, qkv, cotb, scores, mixl, dmix, d_all, d_oth, att_oth, att_snd,
    st_snd, st_rcv, bk_snd, bk_rcv, prior, later,
    p0, p1, p2, sa, ra, sb, rb, sc, rc, acc_a, acc_b, acc_c,
    sa_y, ra_y, sa_x, ra_x, acc_a2, sb_y, rb_y, sb_z, rb_z, acc_b2, sc_x, rc_x, sc_z, rc_z, acc_c2,
    fin, fin_oth, send_sems, recv_sems, loc_sems,
):
    rep, seq = lax.axis_index("rep"), lax.axis_index("seq")
    z, yh = lax.div(rep, jnp.int32(2)), mod(rep, 2)
    x, yl, c = lax.div(seq, jnp.int32(4)), mod(lax.div(seq, jnp.int32(2)), 2), mod(seq, 2)
    y = yh * 2 + yl
    oc, oyh = 1 - c, 1 - yh

    def dev(x_, y_, z_, c_):
        return {"rep": z_ * 2 + lax.div(y_, jnp.int32(2)), "seq": x_ * 4 + mod(y_, 2) * 2 + c_}

    def xd(k):
        return dev(mod(x + k, 4), y, z, c)

    def yd(k):
        return dev(x, mod(y + k, 4), z, c)

    def zd(k):
        return dev(x, y, mod(z + k, 8), c)

    partner = dev(x, y, z, oc)
    across = dev(x, 3 - y, z, c)
    group = [(dx, dl) for dx in range(4) for dl in range(2) if dx or dl]

    def gd(dx, dl):
        return dev(mod(x + dx, 4), yh * 2 + mod(yl + dl, 2), z, c)

    def place(dx, dl):
        return mod(x + dx, 4) * 2 + mod(yl + dl, 2)

    here = x * 2 + yl
    xm, xp = mod(x + 3, 4), mod(x + 1, 4)
    ym, yp = mod(y + 3, 4), mod(y + 1, 4)
    ymh, yml, yph, ypl = lax.div(ym, jnp.int32(2)), mod(ym, 2), lax.div(yp, jnp.int32(2)), mod(yp, 2)
    lane_c = pl.ds(pl.multiple_of(c * HD, HD), HD)
    lane_o = pl.ds(pl.multiple_of(oc * HD, HD), HD)
    mine = pl.ds(pl.multiple_of(c * 512, 512), 512)

    def cols(p):
        return pl.ds(pl.multiple_of(mod(z + OFF[p], 8) * 512, 512), 512)

    peers = [partner] + [xd(k) for k in (1, 2, 3)] + [yd(k) for k in (1, 2, 3)] + [zd(k) for k in range(1, 8)]
    peers += [gd(dx, 1) for dx in (1, 2, 3)]
    bar = pltpu.get_barrier_semaphore()
    for to in peers:
        pl.semaphore_signal(bar, inc=1, device_id=to, device_id_type=MESH)
    loads = [
        pltpu.make_async_copy(src, dst, loc_sems.at[i])
        for i, (src, dst) in enumerate(
            (
                (wk.at[x, yl, :, lane_c], w1.at[0, yh, x, yl]),
                (wv.at[x, yl, :, lane_c], w2.at[0, yh, x, yl]),
                (wq.at[:, :, :, lane_c], w0.at[0, yh]),
                (tok_hbm, tok.at[mine]),
                (cot.at[:, lane_c], cotb.at[c]),
            )
        )
    ]
    for cp in loads:
        cp.start()
    for cp in loads[:3]:
        cp.wait()
    pl.semaphore_wait(bar, len(peers))

    net = Net(send_sems, recv_sems)

    b_z, c_z = {}, {}
    for k in (1, 7, 2, 6, 3, 5, 4):
        to = SLOT[back(k)]
        b_z[k] = net.send(w1.at[0, yh, x, yl], w1.at[to, yh, x, yl], zd(k))
        c_z[k] = net.send(w2.at[0, yh, x, yl], w2.at[to, yh, x, yl], zd(k))

    def a_send(half, k, way):
        at, to = (back(k), back(k + 1)) if way == 0 else (k, k + 1)
        return net.send(w0.at[SLOT[at], half], w0.at[SLOT[to], half], zd(1 if way == 0 else 7))

    def slots(g):
        return pl.ds(g[0], g[1] - g[0])

    def b_y(g):
        ref = w1.at[slots(g), yh, x, yl]
        return [net.send(ref, ref, yd(k)) for k in (1, 3, 2)]

    def c_x(g):
        ref = w2.at[slots(g), yh, x, yl]
        return [net.send(ref, ref, xd(k)) for k in (1, 3, 2)]

    def wait(cps):
        for cp in cps:
            cp.wait_recv()

    def z_wait(g):
        for p in range(*g):
            b_z[back(OFF[p])].wait_recv()
            c_z[back(OFF[p])].wait_recv()

    def b_x(g, prev):
        wait(prev)
        ref = [w1.at[slots(g), h, x] for h in (0, 1)]
        return [net.send(ref[h], ref[h], xd(k)) for h, k in ((0, 1), (1, 3), (1, 1), (0, 3))]

    def c_y(g, prev):
        wait(prev)
        ref = [w2.at[slots(g), yh, pl.ds(2 * h, 2), yl] for h in (0, 1)]
        return [net.send(ref[h], ref[h], yd(k)) for h, k in ((0, 1), (1, 3), (1, 1), (0, 3))]

    def b_f(g, prev):
        prev[0].wait_recv()
        ref = w1.at[slots(g), 0, xm]
        out = [net.send(ref, ref, xd(1))]
        prev[1].wait_recv()
        ref = w1.at[slots(g), 1, xp]
        return prev[2:] + out + [net.send(ref, ref, xd(3))]

    def c_f(g, prev):
        prev[0].wait_recv()
        ref = w2.at[slots(g), ymh, pl.ds(0, 2), yml]
        out = [net.send(ref, ref, yd(1))]
        prev[1].wait_recv()
        ref = w2.at[slots(g), yph, pl.ds(2, 2), ypl]
        return prev[2:] + out + [net.send(ref, ref, yd(3))]

    ga, gb, gc, ge = GROUPS
    b1, c1 = [b_y(ga)], [c_x(ga)]
    a_y = net.send(w0.at[0, yh], w0.at[0, yh], across)
    a1 = [a_send(yh, 0, 0), a_send(yh, 0, 1)]
    cot_x = net.send(cot.at[:, lane_o], cotb.at[c], partner)
    tok_x = net.send(tok_hbm, tok.at[mine], partner)

    def a_step(prev, k):
        out = []
        for i, half in ((0, yh), (2, oyh)):
            prev[i].wait_recv()
            out.append(a_send(half, k, 0))
            prev[i + 1].wait_recv()
            out.append(a_send(half, k, 1))
        return out

    def project(ps, lanes, ws, first):
        @pl.loop(0, 2)
        def _(i):
            r = pl.ds(pl.multiple_of(i * 512, 512), 512)
            got = None
            for p in ps:
                w = jnp.concatenate([w[p].reshape(512, HD) for w in ws], 1)
                term = dot(tok[r, cols(p)], w)
                got = term if got is None else got + term
            acc[r, lanes] = got if first else acc[r, lanes] + got

    def q_acc(*ps):
        project(ps, slice(0, 128), (w0,), ps[0] == 0)

    def kv_acc(g):
        project(range(*g), slice(128, 384), (w1, w2), g[0] == 0)

    z_wait(gb)
    b1.append(b_y(gb))
    c1.append(c_x(gb))
    a_y.wait_recv()
    a1 += [a_send(oyh, 0, 0), a_send(oyh, 0, 1)]
    b2, c2 = [b_x(ga, b1[0])], [c_y(ga, c1[0])]
    z_wait(gc)
    b1.append(b_y(gc))
    c1.append(c_x(gc))
    a2 = a_step(a1, 1)
    b2.append(b_x(gb, b1[1]))
    c2.append(c_y(gb, c1[1]))
    z_wait(ge)
    b1.append(b_y(ge))
    c1.append(c_x(ge))
    b3, c3 = [b_f(ga, b2[0])], [c_f(ga, c2[0])]
    b2.append(b_x(gc, b1[2]))
    c2.append(c_y(gc, c1[2]))
    a3 = a_step(a2, 2)
    b3.append(b_f(gb, b2[1]))
    c3.append(c_f(gb, c2[1]))
    b2.append(b_x(ge, b1[3]))
    c2.append(c_y(ge, c1[3]))
    loads[3].wait()
    tok_x.wait_recv()
    q_acc(0)
    wait(b3[0] + c3[0])
    kv_acc(ga)
    b3.append(b_f(gc, b2[2]))
    c3.append(c_f(gc, c2[2]))
    q_acc(1, 2)
    wait(a3)
    a4 = [a_send(0, 3, 0), a_send(1, 3, 1)]
    wait(b3[1] + c3[1])
    kv_acc(gb)
    q_acc(3, 4)
    b3.append(b_f(ge, b2[3]))
    c3.append(c_f(ge, c2[3]))
    wait(b3[2] + c3[2])
    kv_acc(gc)
    q_acc(5, 6)
    wait(b3[3] + c3[3])
    w_x = [net.send(w1, o1, partner), net.send(w2, o2, partner)]
    kv_acc(ge)

    rows = [slice(0, 512), slice(512, 1024)]
    state = []
    for r in rows:
        qkv[r, 128:384] = acc[r, 128:384].astype(bf16)
        state.append(dot(qkv[r, 128:256], qkv[r, 256:384], 0, 0))
    st_snd[...] = (state[0] + state[1]).astype(bf16)
    prior[0] = jnp.zeros((HD, HD), f32)
    prior[1] = state[0]
    st = [net.send_if(place(dx, dl) > here, st_snd, st_rcv.at[i], gd(dx, dl)) for i, (dx, dl) in enumerate(group)]

    wait(a4)
    w_x.append(net.send(w0, o0, partner))
    q_acc(7)
    qkv[:, 0:128] = acc[:, 0:128].astype(bf16)
    causal = lax.broadcasted_iota(jnp.int32, (512, 512), 0) >= lax.broadcasted_iota(jnp.int32, (512, 512), 1)
    for b, r in enumerate(rows):
        scores[b] = jnp.where(causal, dot(qkv[r, 0:128], qkv[r, 128:256], 1, 1), 0.0).astype(bf16)
        mixl[b] = dot(scores[b], qkv[r, 256:384])
    loads[4].wait()
    cot_x.wait_recv()
    for i, (dx, dl) in enumerate(group):

        @pl.when(place(4 - dx, dl) < here)
        def _(i=i):
            st[i].wait_recv()
            got = st_rcv[i].astype(f32)
            prior[0] += got
            prior[1] += got

    back_state = []
    for b, r in enumerate(rows):
        p_hi, p_lo = split(prior[b])
        q = qkv[r, 0:128]
        mix = mixl[b] + (dot(q, p_hi) + dot(q, p_lo))
        s = lax.rsqrt(jnp.mean(mix * mix, -1, keepdims=True) + EPS)
        att_snd[b] = (mix * s).astype(bf16)
        g = cotb[b].astype(f32)
        m = jnp.mean(g * mix, -1, keepdims=True)
        dmix[b] = (s * g - s * s * s * mix * m).astype(bf16)
        back_state.append(dot(q, dmix[b], 0, 0))
    bk_snd[...] = (back_state[0] + back_state[1]).astype(bf16)
    later[1] = jnp.zeros((HD, HD), f32)
    later[0] = back_state[1]
    bk = [net.send_if(place(dx, dl) < here, bk_snd, bk_rcv.at[i], gd(dx, dl)) for i, (dx, dl) in enumerate(group)]
    att_x = net.send(att_snd.at[oc], att_oth, partner)
    att_o[:, lane_c] = att_snd[c]

    d_loc = []
    for b, r in enumerate(rows):
        q, k, v = qkv[r, 0:128], qkv[r, 128:256], qkv[r, 256:384]
        bs = jnp.where(causal, dot(dmix[b], v, 1, 1), 0.0).astype(bf16)
        p_hi, p_lo = split(prior[b])
        d_all[r, 0:128] = (dot(bs, k) + (dot(dmix[b], p_hi, 1, 1) + dot(dmix[b], p_lo, 1, 1))).astype(bf16)
        mixl[b] = dot(bs, q, 0, 0)
        d_loc.append(dot(scores[b], dmix[b], 0, 0))

    def p_q(p):
        p0[p] = dot(tok[:, cols(p)], d_all[:, 0:128], 0, 0).reshape(BLK[1:])

    def p_kv(g):
        for p in range(*g):
            got = dot(tok[:, cols(p)], d_all[:, 128:384], 0, 0)
            p1[p] = got[:, 0:128].reshape(BLK[1:])
            p2[p] = got[:, 128:256].reshape(BLK[1:])

    def p_qkv(g):
        for p in range(*g):
            got = dot(tok[:, cols(p)], d_all[...], 0, 0)
            p0[p] = got[:, 0:128].reshape(BLK[1:])
            p1[p] = got[:, 128:256].reshape(BLK[1:])
            p2[p] = got[:, 256:384].reshape(BLK[1:])

    def a_out(way, step, half, plus):
        k = 5 - step
        val = p0[SLOT[k if way == 0 else 8 - k], half]
        if plus is not None:
            plus.wait_recv()
            val = val + ra[way, step - 2, half].astype(f32)
        sa[way, step - 1, half] = val.astype(bf16)
        return net.send(sa.at[way, step - 1, half], ra.at[way, step - 1, half], zd(1 if way == 0 else 7))

    p_q(7)
    r1 = [a_out(0, 1, 0, None), a_out(1, 1, 1, None)]
    p_q(5)
    r2r = [None, a_out(0, 2, 1, None)]
    p_q(6)
    r2l = [a_out(1, 2, 0, None), None]
    p_q(3)
    p_q(4)
    r2r[0] = a_out(0, 2, 0, r1[0])
    r2l[1] = a_out(1, 2, 1, r1[1])

    for i, (dx, dl) in enumerate(group):

        @pl.when(place(4 - dx, dl) > here)
        def _(i=i):
            bk[i].wait_recv()
            got = bk_rcv[i].astype(f32)
            later[0] += got
            later[1] += got

    for b, r in enumerate(rows):
        l_hi, l_lo = split(later[b])
        k, v = qkv[r, 128:256], qkv[r, 256:384]
        d_all[r, 128:256] = (mixl[b] + (dot(v, l_hi, 1, 1) + dot(v, l_lo, 1, 1))).astype(bf16)
        d_all[r, 256:384] = (d_loc[b] + (dot(k, l_hi) + dot(k, l_lo))).astype(bf16)
    d_x = net.send(d_all.at[pl.ds(pl.multiple_of(oc * 512, 512), 512)], d_oth, partner)

    r3r = [None, a_out(0, 3, 1, r2r[1])]
    r3l = [a_out(1, 3, 0, r2l[0]), None]

    def b_out(g, way, step, h, plus):
        k = 3 - step
        at = mod(x + (k if way == 0 else 4 - k), 4)
        val = p1[slots(g), h, at]
        if plus is not None:
            plus.wait_recv()
            val = val + rb[way, 0, slots(g), h].astype(f32)
        sb[way, step - 1, slots(g), h] = val.astype(bf16)
        return net.send(sb.at[way, step - 1, slots(g), h], rb.at[way, step - 1, slots(g), h], xd(1 if way == 0 else 3))

    def c_out(g, way, step, h, plus):
        k = 3 - step
        at = mod(y + (k if way == 0 else 4 - k), 4)
        part = pl.ds(2 * h, 2)
        val = p2[slots(g), lax.div(at, jnp.int32(2)), part, mod(at, 2)]
        if plus is not None:
            plus.wait_recv()
            val = val + rc[way, 0, slots(g), part].astype(f32)
        sc[way, step - 1, slots(g), part] = val.astype(bf16)
        return net.send(
            sc.at[way, step - 1, slots(g), part], rc.at[way, step - 1, slots(g), part], yd(1 if way == 0 else 3)
        )

    def first(g):
        return [
            [f(g, 0, 1, 0, None), f(g, 1, 1, 1, None), f(g, 0, 2, 1, None), f(g, 1, 2, 0, None)] for f in (b_out, c_out)
        ]

    def second(g, prev):
        return [
            q[2:] + [f(g, 0, 2, 0, q[0]), f(g, 1, 2, 1, q[1])] for f, q in zip((b_out, c_out), prev)
        ]

    def third(g, prev):
        wait(prev[0])
        acc_b[slots(g)] = p1[slots(g), :, x] + rb[0, 1, slots(g)].astype(f32) + rb[1, 1, slots(g)].astype(f32)
        out = [[], []]
        for k in (2, 1, 3):
            at = mod(y + k, 4)
            sb_y[k - 1, slots(g)] = acc_b[slots(g), lax.div(at, jnp.int32(2)), mod(at, 2)].astype(bf16)
            out[0].append(net.send(sb_y.at[k - 1, slots(g)], rb_y.at[k - 1, slots(g)], yd(k)))
        wait(prev[1])
        acc_c[slots(g)] = p2[slots(g), yh, :, yl] + rc[0, 1, slots(g)].astype(f32) + rc[1, 1, slots(g)].astype(f32)
        for k in (2, 1, 3):
            sc_x[k - 1, slots(g)] = acc_c[slots(g), mod(x + k, 4)].astype(bf16)
            out[1].append(net.send(sc_x.at[k - 1, slots(g)], rc_x.at[k - 1, slots(g)], xd(k)))
        return out

    b_last, c_last = [], []

    def fourth(g, prev):
        wait(prev[0])
        acc_b2[slots(g)] = acc_b[slots(g), yh, yl] + sum(rb_y[k, slots(g)].astype(f32) for k in range(3))
        wait(prev[1])
        acc_c2[slots(g)] = acc_c[slots(g), x] + sum(rc_x[k, slots(g)].astype(f32) for k in range(3))
        for p in range(*g):
            k = OFF[p]
            if k:
                to = SLOT[back(k)]
                sb_z[p] = acc_b2[p].astype(bf16)
                sc_z[p] = acc_c2[p].astype(bf16)
                b_last.append(net.send(sb_z.at[p], rb_z.at[to], zd(k)))
                c_last.append(net.send(sc_z.at[p], rc_z.at[to], zd(k)))

    p_kv(ge)
    f_e = first(ge)
    p_kv(gc)
    f_c = first(gc)
    r3r[0] = a_out(0, 3, 0, r2r[0])
    r3l[1] = a_out(1, 3, 1, r2l[1])
    p_qkv(gb)
    f_b = first(gb)
    s_e = second(ge, f_e)
    r4 = [a_out(0, 4, 1, r3r[1]), a_out(1, 4, 0, r3l[0])]
    p_qkv(ga)
    f_a = first(ga)
    s_c = second(gc, f_c)
    r4 += [a_out(0, 4, 0, r3r[0]), a_out(1, 4, 1, r3l[1])]

    def g_t(*ps):
        for p in ps:
            w = jnp.concatenate([ref[p].reshape(512, HD) for ref in (w0, w1, w2, o0, o1, o2)], 1)
            d = jnp.concatenate([d_all[mine, :], d_oth[...]], 1)
            gt_o[:, cols(p)] = dot(d, w, 1, 1).astype(bf16)

    s_b = second(gb, f_b)
    t_e = third(ge, s_e)
    s_a = second(ga, f_a)
    d_x.wait_recv()
    wait(w_x)
    g_t(0, 1)
    t_c = third(gc, s_c)
    wait(r4)
    acc_a[...] = p0[0] + ra[0, 3].astype(f32) + ra[1, 3].astype(f32)
    a_y2 = []
    for k in (2, 1, 3):
        at = mod(y + k, 4)
        sa_y[k - 1] = acc_a[lax.div(at, jnp.int32(2)), :, mod(at, 2)].astype(bf16)
        a_y2.append(net.send(sa_y.at[k - 1], ra_y.at[k - 1], yd(k)))
    fourth(ge, t_e)
    g_t(2, 3)
    t_b = third(gb, s_b)
    fourth(gc, t_c)
    wait(a_y2)
    acc_a2[...] = acc_a[yh, :, yl] + sum(ra_y[k].astype(f32) for k in range(3))
    a_x2 = []
    for k in (2, 1, 3):
        sa_x[k - 1] = acc_a2[mod(x + k, 4)].astype(bf16)
        a_x2.append(net.send(sa_x.at[k - 1], ra_x.at[k - 1], xd(k)))
    t_a = third(ga, s_a)
    g_t(4, 5)
    fourth(gb, t_b)
    g_t(6, 7)
    att_x.wait_recv()
    att_o[:, lane_o] = att_oth[...]
    wait(a_x2)
    scale = 1.0 / T_DEV
    fin[0] = ((acc_a2[x] + sum(ra_x[k].astype(f32) for k in range(3))) * scale).reshape(2, 16, HD)
    fourth(ga, t_a)
    wait(b_last)
    fin[1] = ((acc_b2[0] + sum(rb_z[k].astype(f32) for k in range(1, 8))) * scale).reshape(2, 16, HD)
    wait(c_last)
    fin[2] = ((acc_c2[0] + sum(rc_z[k].astype(f32) for k in range(1, 8))) * scale).reshape(2, 16, HD)
    fin_x = net.send(fin.at[:, oc], fin_oth, partner)
    for i, o in enumerate((gq_o, gk_o, gv_o)):
        o[:, lane_c] = fin[i, c]
    fin_x.wait_recv()
    for i, o in enumerate((gq_o, gk_o, gv_o)):
        o[:, lane_o] = fin_oth[i]
    net.finish()


def write_out(*refs):
    sems = refs[10]
    copies = [pltpu.make_async_copy(refs[i], refs[5 + i], sems.at[i]) for i in (1, 0, 2, 3, 4)]
    for cp in copies:
        cp.start()
    for cp in copies:
        cp.wait()


def body(tokens, w_query, w_key, w_value, cotangent):
    vm, any_ = pl.BlockSpec(memory_space=pltpu.VMEM), pl.BlockSpec(memory_space=pl.ANY)
    hbm = pl.BlockSpec(memory_space=pltpu.HBM)

    def v(*shape, t=bf16):
        return pltpu.VMEM(shape, t)

    scratch = [v(1024, D)] + [v(*BLK)] * 6
    scratch += [v(1024, 384, t=f32), v(1024, 384), v(2, 512, 128), v(2, 512, 512), v(2, 512, 128, t=f32), v(2, 512, 128)]
    scratch += [v(1024, 384), v(512, 384), v(512, 128), v(2, 512, 128)]
    scratch += [v(128, 128), v(7, 128, 128), v(128, 128), v(7, 128, 128), v(2, 128, 128, t=f32), v(2, 128, 128, t=f32)]
    scratch += [v(*BLK, t=f32)] * 3
    scratch += [v(2, 4, 2, 4, 2, 32, 128)] * 2 + [v(2, 2, 8, 2, 2, 32, 128)] * 2 + [v(2, 2, 8, 4, 32, 128)] * 2
    scratch += [v(2, 4, 2, 32, 128, t=f32), v(8, 2, 2, 32, 128, t=f32), v(8, 4, 32, 128, t=f32)]
    scratch += [v(3, 4, 32, 128)] * 2 + [v(3, 32, 128)] * 2 + [v(4, 32, 128, t=f32)]
    scratch += [v(3, 8, 32, 128)] * 2 + [v(8, 32, 128)] * 2 + [v(8, 32, 128, t=f32)]
    scratch += [v(3, 8, 32, 128)] * 2 + [v(8, 32, 128)] * 2 + [v(8, 32, 128, t=f32)]
    scratch += [v(3, 2, 16, 128, t=f32), v(3, 16, 128, t=f32)]
    scratch += [pltpu.SemaphoreType.DMA((N_SEM,)), pltpu.SemaphoreType.DMA((N_SEM,)), pltpu.SemaphoreType.DMA((5,))]
    grad = pltpu.VMEM((16, 256), f32)
    args = [tokens] + [w.reshape(4, 2, 32, 256) for w in (w_query, w_key, w_value)] + [cotangent]
    outs = pl.pallas_call(
        kernel,
        out_shape=(
            pltpu.VMEM((T_DEV, 256), bf16),
            pltpu.VMEM((T_DEV, D), bf16),
            grad,
            grad,
            grad,
        ),
        in_specs=[hbm] * 5,
        out_specs=(vm, vm, vm, vm, vm),
        scratch_shapes=scratch,
        compiler_params=pltpu.CompilerParams(collective_id=0, has_side_effects=True, vmem_limit_bytes=48 * 2**20),
        cost_estimate=pl.CostEstimate(flops=10**10, bytes_accessed=10**7, transcendentals=1024),
        name="step",
    )(*[pltpu.with_memory_space_constraint(a, pltpu.HBM) for a in args])
    return pl.pallas_call(
        write_out,
        out_shape=[jax.ShapeDtypeStruct(o.shape, o.dtype) for o in outs],
        in_specs=[vm] * 5,
        out_specs=[any_] * 5,
        scratch_shapes=[pltpu.SemaphoreType.DMA((5,))],
        compiler_params=pltpu.CompilerParams(vmem_limit_bytes=2**20),
        name="write_out",
    )(*[pltpu.with_memory_space_constraint(o, pltpu.VMEM) for o in outs])


def solution(mesh):
    both = P(("rep", "seq"), None)
    rep = P("rep", None)
    return jax.shard_map(
        body, mesh=mesh, in_specs=(both, rep, rep, rep, both), out_specs=(both,) * 5, check_vma=False
    )
```

time: 90 us -> 76.5 us (0.85)
  local copies, waits for them, and re-layouts: 8.22 us -> 0 us
  Pallas kernels: 81 us -> 75.6 us
    unnamed x11 -> x0, local copies, waits for them, and re-layouts: 8.22 us -> none
    pallas_call x1 -> x2, Pallas kernels: 81 us -> 75.6 us  [the longest x1 73.5 us: body(): pl.pallas_call(kernel, out_shape=(pltpu.VMEM((T_DEV, 256), bf16), pltpu.V...]
where the time goes in v2:
time: 76.5 us; the launch traced here: 76.4 us
  Pallas kernels  75.6 us (99%)
  between operations  0.8 us (1%)
    pallas_call x1, Pallas kernels, body(): pl.pallas_call(kernel, out_shape=(pltpu.VMEM((T_DEV, 256), bf16), pltpu.V...  73.5 us
    pallas_call x1, Pallas kernels, body(): pl.pallas_call(write_out, out_shape=[jax.ShapeDtypeStruct(o.shape, o.dtyp...  2.14 us

profile of v2, /device:TPU:1, one launch (start us, length us, event | category | flops | bytes accessed | tf_op | source)
XLA Modules:
  0.0 76.4 jit_solution(3006382180984059535)
XLA Ops:
  0.6 73.5 %step.1 = (bf16[512,256]{1,0:T(8,128)(2,1)S(1)}, bf16[512,4096]{1,0:T(8,128)(2,1)S(1)}, f32[16,256]{1,0:T(8,128)S(1)}, f32[16,256]{1,0:T(8,128)S(1)}, f32[16,256]{1,0:T(8,128)S(1)}) custom-call(bf16[512,4096]{1,0:T(8,128)(2,1)} %tok_hbm.1, bf16[4,2,32,256]{3,2,1,0:T(8,128)(2,1)} %bitcast.3, bf16[4,2,32,256]{3,2,1,0:T(8,128)(2,1)} %bitcast.4, ...), custom_call_target="tpu_custom_call" | custom-call | flops 10000000000 | bytes 10000000 | tf_op jit(solution)/shard_map/step/pallas_call | solution.py:552
  74.1 2.1 %write_out.1 = (bf16[512,256]{1,0:T(8,128)(2,1)}, bf16[512,4096]{1,0:T(8,128)(2,1)}, f32[16,256]{1,0:T(8,128)}, f32[16,256]{1,0:T(8,128)}, f32[16,256]{1,0:T(8,128)}) custom-call(bf16[512,256]{1,0:T(8,128)(2,1)S(1)} %get-tuple-element.10.refs_0_, bf16[512,4096]{1,0:T(8,128)(2,1)S(1)} %get-tuple-element.11.refs_1_, f32[16,256]{1,0:T(8,128)S(1)} %get-tuple-element.12.refs_2_, ...), custom_call_target="tpu_custom_call" | custom-call | tf_op jit(solution)/shard_map/write_out/pallas_call | solution.py:568

commit v3 on v2

v3 whole, which is shorter than its diff:
```python
import math

import jax
import jax.numpy as jnp
from jax import lax
from jax.experimental import pallas as pl
from jax.experimental.pallas import tpu as pltpu
from jax.sharding import PartitionSpec as P

D = 4096
HD = 128
T_DEV = 512
EPS = 1e-06
MESH = pl.DeviceIdType.MESH
f32 = jnp.float32
bf16 = jnp.bfloat16
N_SEM = 64
BLK = (8, 2, 4, 2, 32, 128)


def mod(a, n):
    return lax.rem(a, jnp.int32(n))


def dot(a, b, ca=1, cb=0):
    return lax.dot_general(a, b, (((ca,), (cb,)), ((), ())), preferred_element_type=f32)


def split(a):
    hi = a.astype(bf16)
    return hi, (a - hi.astype(f32)).astype(bf16)


class Batch:
    def __init__(self, net):
        self.net, self.i, self.copies, self.units = net, net.n, [], 0
        net.n += 1
        assert net.n <= N_SEM
        net.batches.append(self)

    def send(self, src, dst, to):
        cp = self.net.make(src, dst, to, self.i)
        cp.start()
        self.copies.append(cp)
        self.units += math.prod(src.shape) // 2048

    def all(self):
        if len(self.copies) == 1:
            return self.copies[0]
        ref = self.net.sizes.at[pl.ds(0, self.units)]
        return self.net.make(ref, ref, self.net.anyone, self.i)

    def wait(self):
        self.all().wait_recv()


class Net:
    def __init__(self, send_sems, recv_sems, sizes, anyone):
        self.ss, self.rs, self.sizes, self.anyone = send_sems, recv_sems, sizes, anyone
        self.n, self.batches, self.maybe = 0, [], []

    def make(self, src, dst, to, i):
        return pltpu.make_async_remote_copy(
            src_ref=src, dst_ref=dst, send_sem=self.ss.at[i], recv_sem=self.rs.at[i], device_id=to, device_id_type=MESH
        )

    def one(self, src, dst, to):
        b = Batch(self)
        b.send(src, dst, to)
        return b

    def some(self, sends):
        b = Batch(self)
        for src, dst, to in sends:
            b.send(src, dst, to)
        return b

    def send_if(self, cond, src, dst, to, i):
        cp = self.make(src, dst, to, i)
        pl.when(cond)(cp.start)
        self.maybe.append((cp, cond))
        return cp

    def finish(self):
        for b in self.batches:
            b.all().wait_send()
        for cp, cond in self.maybe:
            pl.when(cond)(cp.wait_send)


OFF = (0, 1, 7, 2, 6, 3, 5, 4)
SLOT = {k: p for p, k in enumerate(OFF)}
GROUPS = ((0, 1), (1, 3), (3, 5), (5, 8))


def back(k):
    return (8 - k) % 8


def kernel(
    tok_hbm, wq, wk, wv, cot, att_o, gt_o, gq_o, gk_o, gv_o,
    tok, w0, w1, w2, o0, o1, o2, acc, qkv, cotb, scores, mixl, d_loc, dmix, d_all, d_oth, att_oth, att_snd,
    st_snd, st_rcv, bk_snd, bk_rcv, prior, later,
    p0, p1, p2, sa, ra, acc_a, acc_b, acc_c,
    sa_y, ra_y, sa_x, ra_x, acc_a2, sb_y, rb_y, sb_z, rb_z, acc_b2, sc_x, rc_x, sc_z, rc_z, acc_c2,
    sb_d, rb_d, sc_d, rc_d, sizes, send_sems, recv_sems, loc_sems,
):
    rep, seq = lax.axis_index("rep"), lax.axis_index("seq")
    z, yh = lax.div(rep, jnp.int32(2)), mod(rep, 2)
    x, yl, c = lax.div(seq, jnp.int32(4)), mod(lax.div(seq, jnp.int32(2)), 2), mod(seq, 2)
    y = yh * 2 + yl
    oc, oyh = 1 - c, 1 - yh

    def dev(x_, y_, z_, c_):
        return {"rep": z_ * 2 + lax.div(y_, jnp.int32(2)), "seq": x_ * 4 + mod(y_, 2) * 2 + c_}

    def xd(k):
        return dev(mod(x + k, 4), y, z, c)

    def yd(k):
        return dev(x, mod(y + k, 4), z, c)

    def zd(k):
        return dev(x, y, mod(z + k, 8), c)

    partner = dev(x, y, z, oc)
    across = dev(x, 3 - y, z, c)
    group = [(dx, dl) for dx in range(4) for dl in range(2) if dx or dl]

    def gd(dx, dl):
        return dev(mod(x + dx, 4), yh * 2 + mod(yl + dl, 2), z, c)

    def place(dx, dl):
        return mod(x + dx, 4) * 2 + mod(yl + dl, 2)

    here = x * 2 + yl
    xm, xp = mod(x + 3, 4), mod(x + 1, 4)
    ym, yp = mod(y + 3, 4), mod(y + 1, 4)
    ymh, yml, yph, ypl = lax.div(ym, jnp.int32(2)), mod(ym, 2), lax.div(yp, jnp.int32(2)), mod(yp, 2)
    lane_c = pl.ds(pl.multiple_of(c * HD, HD), HD)
    lane_o = pl.ds(pl.multiple_of(oc * HD, HD), HD)
    mine = pl.ds(pl.multiple_of(c * 512, 512), 512)

    def cols(p):
        return pl.ds(pl.multiple_of(mod(z + OFF[p], 8) * 512, 512), 512)

    peers = [partner] + [xd(k) for k in (1, 2, 3)] + [yd(k) for k in (1, 2, 3)] + [zd(k) for k in range(1, 8)]
    peers += [gd(dx, 1) for dx in (1, 2, 3)]
    peers += [dev(mod(x + k, 4), y, z, oc) for k in (1, 2, 3)] + [dev(x, y, mod(z + k, 8), oc) for k in range(1, 8)]
    bar = pltpu.get_barrier_semaphore()
    for to in peers:
        pl.semaphore_signal(bar, inc=1, device_id=to, device_id_type=MESH)
    loads = [
        pltpu.make_async_copy(src, dst, loc_sems.at[i])
        for i, (src, dst) in enumerate(
            (
                (wk.at[x, yl, :, lane_c], w1.at[0, yh, x, yl]),
                (wv.at[x, yl, :, lane_c], w2.at[0, yh, x, yl]),
                (wq.at[:, :, :, lane_c], w0.at[0, yh]),
                (tok_hbm, tok.at[mine]),
                (cot.at[:, lane_c], cotb.at[c]),
            )
        )
    ]
    for cp in loads:
        cp.start()
    for cp in loads[:3]:
        cp.wait()
    pl.semaphore_wait(bar, len(peers))

    net = Net(send_sems, recv_sems, sizes, partner)

    ga, gb, gc, ge = GROUPS
    steps = {g: Batch(net) for g in GROUPS[1:]}
    for k in (1, 7, 2, 6, 3, 5, 4):
        to = SLOT[back(k)]
        for g in GROUPS[1:]:
            if to in range(*g):
                for w in (w1, w2):
                    steps[g].send(w.at[0, yh, x, yl], w.at[to, yh, x, yl], zd(k))

    def slots(g):
        return pl.ds(g[0], g[1] - g[0])

    def mid(g):
        if g in steps:
            steps[g].wait()
        b, c_ = w1.at[slots(g), yh, x, yl], w2.at[slots(g), yh, x, yl]
        return net.some([t for k in (1, 3, 2) for t in ((b, b, yd(k)), (c_, c_, xd(k)))])

    def wide(g, prev):
        prev.wait()
        b = [w1.at[slots(g), h, x] for h in (0, 1)]
        c_ = [w2.at[slots(g), yh, pl.ds(2 * h, 2), yl] for h in (0, 1)]
        lead = net.some([t for h, k in ((0, 1), (1, 3)) for t in ((b[h], b[h], xd(k)), (c_[h], c_[h], yd(k)))])
        rest = net.some([t for h, k in ((1, 1), (0, 3)) for t in ((b[h], b[h], xd(k)), (c_[h], c_[h], yd(k)))])
        return lead, rest

    def pass_on(g, prev):
        lead, rest = prev
        lead.wait()
        for ref, to in (
            (w1.at[slots(g), 0, xm], xd(1)),
            (w1.at[slots(g), 1, xp], xd(3)),
            (w2.at[slots(g), ymh, pl.ds(0, 2), yml], yd(1)),
            (w2.at[slots(g), yph, pl.ds(2, 2), ypl], yd(3)),
        ):
            rest.send(ref, ref, to)
        return rest

    def a_send(k, *parts):
        sends = []
        for half, way in parts:
            at, to = (back(k), back(k + 1)) if way == 0 else (k, k + 1)
            sends.append((w0.at[SLOT[at], half], w0.at[SLOT[to], half], zd(1 if way == 0 else 7)))
        return net.some(sends)

    def a_half(prev, half, k):
        prev.wait()
        return a_send(k, (half, 0), (half, 1))

    m_a = mid(ga)
    a_y = net.one(w0.at[0, yh], w0.at[0, yh], across)
    a1 = [a_send(0, (yh, 0), (yh, 1))]
    cot_x = net.one(cot.at[:, lane_o], cotb.at[c], partner)
    tok_x = net.one(tok_hbm, tok.at[mine], partner)

    def project(ps, lanes, ws, first):
        @pl.loop(0, 2)
        def _(i):
            r = pl.ds(pl.multiple_of(i * 512, 512), 512)
            got = None
            for p in ps:
                w = jnp.concatenate([w[p].reshape(512, HD) for w in ws], 1)
                term = dot(tok[r, cols(p)], w)
                got = term if got is None else got + term
            acc[r, lanes] = got if first else acc[r, lanes] + got

    def q_acc(*ps):
        project(ps, slice(0, 128), (w0,), ps[0] == 0)

    def kv_acc(g):
        project(range(*g), slice(128, 384), (w1, w2), g[0] == 0)

    m_b = mid(gb)
    n_a = wide(ga, m_a)
    a_y.wait()
    a1.append(a_send(0, (oyh, 0), (oyh, 1)))
    m_c = mid(gc)
    m_e = mid(ge)
    n_b = wide(gb, m_b)
    a2 = [a_half(a1[0], yh, 1)]
    f_a = pass_on(ga, n_a)
    n_c = wide(gc, m_c)
    a2.append(a_half(a1[1], oyh, 1))
    n_e = wide(ge, m_e)
    f_b = pass_on(gb, n_b)
    loads[3].wait()
    tok_x.wait()
    f_a.wait()
    kv_acc(ga)
    f_c = pass_on(gc, n_c)
    a3 = [a_half(a2[0], yh, 2)]
    q_acc(0)
    q_acc(1, 2)
    f_e = pass_on(ge, n_e)
    a3.append(a_half(a2[1], oyh, 2))
    f_b.wait()
    kv_acc(gb)
    f_c.wait()
    kv_acc(gc)
    for cp in a3:
        cp.wait()
    a4 = a_send(3, (0, 0), (1, 1))
    f_e.wait()
    w_x = [net.one(w1, o1, partner), net.one(w2, o2, partner)]
    kv_acc(ge)

    rows = [slice(0, 512), slice(512, 1024)]
    state = []
    for r in rows:
        qkv[r, 128:384] = acc[r, 128:384].astype(bf16)
        state.append(dot(qkv[r, 128:256], qkv[r, 256:384], 0, 0))
    st_snd[...] = (state[0] + state[1]).astype(bf16)
    prior[0] = jnp.zeros((HD, HD), f32)
    prior[1] = state[0]
    pair = net.n
    net.n += len(group)
    st = [
        net.send_if(place(dx, dl) > here, st_snd, st_rcv.at[i], gd(dx, dl), pair + i) for i, (dx, dl) in enumerate(group)
    ]

    q_acc(3, 4, 5, 6)
    a4.wait()
    w_x.append(net.one(w0, o0, partner))
    q_acc(7)
    qkv[:, 0:128] = acc[:, 0:128].astype(bf16)
    causal = lax.broadcasted_iota(jnp.int32, (512, 512), 0) >= lax.broadcasted_iota(jnp.int32, (512, 512), 1)
    for b, r in enumerate(rows):
        scores[b] = jnp.where(causal, dot(qkv[r, 0:128], qkv[r, 128:256], 1, 1), 0.0).astype(bf16)
        mixl[b] = dot(scores[b], qkv[r, 256:384])
    loads[4].wait()
    cot_x.wait()
    for i, (dx, dl) in enumerate(group):

        @pl.when(place(4 - dx, dl) < here)
        def _(i=i):
            st[i].wait_recv()
            got = st_rcv[i].astype(f32)
            prior[0] += got
            prior[1] += got

    back_state = []
    for b, r in enumerate(rows):
        p_hi, p_lo = split(prior[b])
        q = qkv[r, 0:128]
        mix = mixl[b] + (dot(q, p_hi) + dot(q, p_lo))
        s = lax.rsqrt(jnp.mean(mix * mix, -1, keepdims=True) + EPS)
        att_snd[b] = (mix * s).astype(bf16)
        g = cotb[b].astype(f32)
        m = jnp.mean(g * mix, -1, keepdims=True)
        dmix[b] = (s * g - s * s * s * mix * m).astype(bf16)
        back_state.append(dot(q, dmix[b], 0, 0))
    bk_snd[...] = (back_state[0] + back_state[1]).astype(bf16)
    later[1] = jnp.zeros((HD, HD), f32)
    later[0] = back_state[1]
    bk = [
        net.send_if(place(dx, dl) < here, bk_snd, bk_rcv.at[i], gd(dx, dl), pair + i) for i, (dx, dl) in enumerate(group)
    ]
    att_x = net.one(att_snd.at[oc], att_oth, partner)

    for b, r in enumerate(rows):
        q, k, v = qkv[r, 0:128], qkv[r, 128:256], qkv[r, 256:384]
        bs = jnp.where(causal, dot(dmix[b], v, 1, 1), 0.0).astype(bf16)
        p_hi, p_lo = split(prior[b])
        d_all[r, 0:128] = (dot(bs, k) + (dot(dmix[b], p_hi, 1, 1) + dot(dmix[b], p_lo, 1, 1))).astype(bf16)
        mixl[b] = dot(bs, q, 0, 0)
        d_loc[b] = dot(scores[b], dmix[b], 0, 0)

    def p_q(p):
        p0[p] = dot(tok[:, cols(p)], d_all[:, 0:128], 0, 0).reshape(BLK[1:])

    def p_kv(g):
        for p in range(*g):
            got = dot(tok[:, cols(p)], d_all[:, 128:384], 0, 0)
            p1[p] = got[:, 0:128].reshape(BLK[1:])
            p2[p] = got[:, 128:256].reshape(BLK[1:])

    def p_qkv(g):
        for p in range(*g):
            got = dot(tok[:, cols(p)], d_all[...], 0, 0)
            p0[p] = got[:, 0:128].reshape(BLK[1:])
            p1[p] = got[:, 128:256].reshape(BLK[1:])
            p2[p] = got[:, 256:384].reshape(BLK[1:])

    def a_out(step, parts, plus=None):
        if plus is not None:
            plus.wait()
        sends = []
        for way, half in parts:
            k = 5 - step
            val = p0[SLOT[k if way == 0 else 8 - k], half]
            if plus is not None:
                val = val + ra[way, step - 2, half].astype(f32)
            sa[way, step - 1, half] = val.astype(bf16)
            sends.append((sa.at[way, step - 1, half], ra.at[way, step - 1, half], zd(1 if way == 0 else 7)))
        return net.some(sends)

    ends, free = ((0, 0), (1, 1)), ((0, 1), (1, 0))
    p_q(7)
    r1 = a_out(1, ends)
    p_q(5)
    p_q(6)
    r2f = a_out(2, free)

    for i, (dx, dl) in enumerate(group):

        @pl.when(place(4 - dx, dl) > here)
        def _(i=i):
            bk[i].wait_recv()
            got = bk_rcv[i].astype(f32)
            later[0] += got
            later[1] += got

    for b, r in enumerate(rows):
        l_hi, l_lo = split(later[b])
        k, v = qkv[r, 128:256], qkv[r, 256:384]
        d_all[r, 128:256] = (mixl[b] + (dot(v, l_hi, 1, 1) + dot(v, l_lo, 1, 1))).astype(bf16)
        d_all[r, 256:384] = (d_loc[b] + (dot(k, l_hi) + dot(k, l_lo))).astype(bf16)
    d_x = net.one(d_all.at[pl.ds(pl.multiple_of(oc * 512, 512), 512)], d_oth, partner)

    def direct(g):
        out = Batch(net)
        for k in (2, 1, 3):
            sb_d[k - 1, slots(g)] = p1[slots(g), :, mod(x + k, 4)].astype(bf16)
            out.send(sb_d.at[k - 1, slots(g)], rb_d.at[k - 1, slots(g)], xd(k))
            at = mod(y + k, 4)
            sc_d[k - 1, slots(g)] = p2[slots(g), lax.div(at, jnp.int32(2)), :, mod(at, 2)].astype(bf16)
            out.send(sc_d.at[k - 1, slots(g)], rc_d.at[k - 1, slots(g)], yd(k))
        return out

    def third(g, prev):
        prev.wait()
        acc_b[slots(g)] = p1[slots(g), :, x] + sum(rb_d[k, slots(g)].astype(f32) for k in range(3))
        acc_c[slots(g)] = p2[slots(g), yh, :, yl] + sum(rc_d[k, slots(g)].astype(f32) for k in range(3))
        out = Batch(net)
        for k in (2, 1, 3):
            at = mod(y + k, 4)
            sb_y[k - 1, slots(g)] = acc_b[slots(g), lax.div(at, jnp.int32(2)), mod(at, 2)].astype(bf16)
            out.send(sb_y.at[k - 1, slots(g)], rb_y.at[k - 1, slots(g)], yd(k))
            sc_x[k - 1, slots(g)] = acc_c[slots(g), mod(x + k, 4)].astype(bf16)
            out.send(sc_x.at[k - 1, slots(g)], rc_x.at[k - 1, slots(g)], xd(k))
        return out

    last = Batch(net)

    def fourth(g, prev):
        prev.wait()
        n = g[1] - g[0]
        got = acc_b[slots(g), yh, yl] + sum(rb_y[k, slots(g)].astype(f32) for k in range(3))
        acc_b2[slots(g)] = got.reshape(n, 2, 16, HD)
        got = acc_c[slots(g), x] + sum(rc_x[k, slots(g)].astype(f32) for k in range(3))
        acc_c2[slots(g)] = got.reshape(n, 2, 16, HD)
        for snd, rcv, total in ((sb_z, rb_z, acc_b2), (sc_z, rc_z, acc_c2)):
            snd[slots(g)] = total[slots(g)].astype(bf16)
            for p in range(*g):
                k = OFF[p]
                to = SLOT[back(k)]
                if k:
                    last.send(snd.at[p, c], rcv.at[0, to], zd(k))
                last.send(snd.at[p, oc], rcv.at[1, to], dev(x, y, mod(z + k, 8), oc) if k else partner)

    def g_t(*ps):
        for p in ps:
            w = jnp.concatenate([ref[p].reshape(512, HD) for ref in (w0, w1, w2, o0, o1, o2)], 1)
            d = jnp.concatenate([d_all[mine, :], d_oth[...]], 1)
            gt_o[:, cols(p)] = dot(d, w, 1, 1).astype(bf16)

    r2 = a_out(2, ends, r1)
    p_kv(ge)
    d_e = direct(ge)
    p_qkv(gc)
    d_c = direct(gc)
    r3f = a_out(3, free, r2f)
    r3 = a_out(3, ends, r2)
    p_qkv(gb)
    d_b = direct(gb)
    p_qkv(ga)
    d_a = direct(ga)
    d_x.wait()
    for cp in w_x:
        cp.wait()
    g_t(0)
    r4f = a_out(4, free, r3f)
    r4 = a_out(4, ends, r3)
    g_t(1, 2)
    t_e = third(ge, d_e)
    t_c = third(gc, d_c)
    g_t(3)
    t_b = third(gb, d_b)
    r4f.wait()
    r4.wait()
    acc_a[...] = p0[0] + ra[0, 3].astype(f32) + ra[1, 3].astype(f32)
    a_y2 = Batch(net)
    for k in (2, 1, 3):
        at = mod(y + k, 4)
        sa_y[k - 1] = acc_a[lax.div(at, jnp.int32(2)), :, mod(at, 2)].astype(bf16)
        a_y2.send(sa_y.at[k - 1], ra_y.at[k - 1], yd(k))
    t_a = third(ga, d_a)
    fourth(ge, t_e)
    g_t(4)
    fourth(gc, t_c)
    fourth(gb, t_b)
    a_y2.wait()
    acc_a2[...] = (acc_a[yh, :, yl] + sum(ra_y[k].astype(f32) for k in range(3))).reshape(4, 2, 16, HD)
    sa_x[...] = acc_a2[...].astype(bf16)
    last.send(sa_x.at[x, oc], ra_x.at[1, 0], partner)
    for k in (2, 1, 3):
        at = mod(x + k, 4)
        last.send(sa_x.at[at, c], ra_x.at[0, k], xd(k))
        last.send(sa_x.at[at, oc], ra_x.at[1, k], dev(at, y, z, oc))
    fourth(ga, t_a)
    g_t(5, 6, 7)
    att_o[:, lane_c] = att_snd[c]
    att_x.wait()
    att_o[:, lane_o] = att_oth[...]
    scale = 1.0 / T_DEV
    last.wait()
    gq_o[:, lane_c] = (acc_a2[x, c] + sum(ra_x[0, k].astype(f32) for k in range(1, 4))) * scale
    gq_o[:, lane_o] = sum(ra_x[1, k].astype(f32) for k in range(4)) * scale
    for out, total, rcv in ((gk_o, acc_b2, rb_z), (gv_o, acc_c2, rc_z)):
        out[:, lane_c] = (total[0, c] + sum(rcv[0, p].astype(f32) for p in range(1, 8))) * scale
        out[:, lane_o] = sum(rcv[1, p].astype(f32) for p in range(8)) * scale
    net.finish()


def write_out(*refs):
    sems = refs[10]
    copies = [pltpu.make_async_copy(refs[i], refs[5 + i], sems.at[i]) for i in (1, 0, 2, 3, 4)]
    for cp in copies:
        cp.start()
    for cp in copies:
        cp.wait()


def body(tokens, w_query, w_key, w_value, cotangent):
    vm, any_ = pl.BlockSpec(memory_space=pltpu.VMEM), pl.BlockSpec(memory_space=pl.ANY)
    hbm = pl.BlockSpec(memory_space=pltpu.HBM)

    def v(*shape, t=bf16):
        return pltpu.VMEM(shape, t)

    scratch = [v(1024, D)] + [v(*BLK)] * 6
    scratch += [v(1024, 384, t=f32), v(1024, 384), v(2, 512, 128), v(2, 512, 512), v(2, 512, 128, t=f32), v(2, 512, 128, t=f32), v(2, 512, 128)]
    scratch += [v(1024, 384), v(512, 384), v(512, 128), v(2, 512, 128)]
    scratch += [v(128, 128), v(7, 128, 128), v(128, 128), v(7, 128, 128), v(2, 128, 128, t=f32), v(2, 128, 128, t=f32)]
    scratch += [v(*BLK, t=f32)] * 3
    scratch += [v(2, 4, 2, 4, 2, 32, 128)] * 2
    scratch += [v(2, 4, 2, 32, 128, t=f32), v(8, 2, 2, 32, 128, t=f32), v(8, 4, 32, 128, t=f32)]
    scratch += [v(3, 4, 32, 128)] * 2 + [v(4, 2, 16, 128), v(2, 4, 16, 128)] + [v(4, 2, 16, 128, t=f32)]
    scratch += [v(3, 8, 32, 128)] * 2 + [v(8, 2, 16, 128), v(2, 8, 16, 128)] + [v(8, 2, 16, 128, t=f32)]
    scratch += [v(3, 8, 32, 128)] * 2 + [v(8, 2, 16, 128), v(2, 8, 16, 128)] + [v(8, 2, 16, 128, t=f32)]
    scratch += [v(3, 8, 2, 2, 32, 128)] * 2 + [v(3, 8, 4, 32, 128)] * 2 + [v(160, 16, 128)]
    scratch += [pltpu.SemaphoreType.DMA((N_SEM,)), pltpu.SemaphoreType.DMA((N_SEM,)), pltpu.SemaphoreType.DMA((5,))]
    grad = pltpu.VMEM((16, 256), f32)
    args = [tokens] + [w.reshape(4, 2, 32, 256) for w in (w_query, w_key, w_value)] + [cotangent]
    outs = pl.pallas_call(
        kernel,
        out_shape=(
            pltpu.VMEM((T_DEV, 256), bf16),
            pltpu.VMEM((T_DEV, D), bf16),
            grad,
            grad,
            grad,
        ),
        in_specs=[hbm] * 5,
        out_specs=(vm, vm, vm, vm, vm),
        scratch_shapes=scratch,
        compiler_params=pltpu.CompilerParams(collective_id=0, has_side_effects=True, vmem_limit_bytes=48 * 2**20),
        cost_estimate=pl.CostEstimate(flops=10**10, bytes_accessed=10**7, transcendentals=1024),
        name="step",
    )(*[pltpu.with_memory_space_constraint(a, pltpu.HBM) for a in args])
    return pl.pallas_call(
        write_out,
        out_shape=[jax.ShapeDtypeStruct(o.shape, o.dtype) for o in outs],
        in_specs=[vm] * 5,
        out_specs=[any_] * 5,
        scratch_shapes=[pltpu.SemaphoreType.DMA((5,))],
        compiler_params=pltpu.CompilerParams(vmem_limit_bytes=2**20),
        name="write_out",
    )(*[pltpu.with_memory_space_constraint(o, pltpu.VMEM) for o in outs])


def solution(mesh):
    both = P(("rep", "seq"), None)
    rep = P("rep", None)
    return jax.shard_map(
        body, mesh=mesh, in_specs=(both, rep, rep, rep, both), out_specs=(both,) * 5, check_vma=False
    )
```

time: 76.5 us -> 68.2 us (0.89)
  Pallas kernels: 75.6 us -> 67.3 us
    pallas_call x1, Pallas kernels: 73.5 us -> 65.2 us  [body(): pl.pallas_call(kernel, out_shape=(pltpu.VMEM((T_DEV, 256), bf16), pltpu.V...]
where the time goes in v3:
time: 68.2 us; the launch traced here: 68.1 us
  Pallas kernels  67.3 us (99%)
  between operations  0.8 us (1%)
    pallas_call x1, Pallas kernels, body(): pl.pallas_call(kernel, out_shape=(pltpu.VMEM((T_DEV, 256), bf16), pltpu.V...  65.2 us
    pallas_call x1, Pallas kernels, body(): pl.pallas_call(write_out, out_shape=[jax.ShapeDtypeStruct(o.shape, o.dtyp...  2.14 us

profile of v3, /device:TPU:1, one launch (start us, length us, event | category | flops | bytes accessed | tf_op | source)
XLA Modules:
  0.0 68.1 jit_solution(6335016984621524925)
XLA Ops:
  0.6 65.2 %step.1 = (bf16[512,256]{1,0:T(8,128)(2,1)S(1)}, bf16[512,4096]{1,0:T(8,128)(2,1)S(1)}, f32[16,256]{1,0:T(8,128)S(1)}, f32[16,256]{1,0:T(8,128)S(1)}, f32[16,256]{1,0:T(8,128)S(1)}) custom-call(bf16[512,4096]{1,0:T(8,128)(2,1)} %tok_hbm.1, bf16[4,2,32,256]{3,2,1,0:T(8,128)(2,1)} %bitcast.3, bf16[4,2,32,256]{3,2,1,0:T(8,128)(2,1)} %bitcast.4, ...), custom_call_target="tpu_custom_call" | custom-call | flops 10000000000 | bytes 10000000 | tf_op jit(solution)/shard_map/step/pallas_call | solution.py:527
  65.8 2.1 %write_out.1 = (bf16[512,256]{1,0:T(8,128)(2,1)}, bf16[512,4096]{1,0:T(8,128)(2,1)}, f32[16,256]{1,0:T(8,128)}, f32[16,256]{1,0:T(8,128)}, f32[16,256]{1,0:T(8,128)}) custom-call(bf16[512,256]{1,0:T(8,128)(2,1)S(1)} %get-tuple-element.10.refs_0_, bf16[512,4096]{1,0:T(8,128)(2,1)S(1)} %get-tuple-element.11.refs_1_, f32[16,256]{1,0:T(8,128)S(1)} %get-tuple-element.12.refs_2_, ...), custom_call_target="tpu_custom_call" | custom-call | tf_op jit(solution)/shard_map/write_out/pallas_call | solution.py:543

commit v4 on v3

--- a/solution.py
+++ b/solution.py
@@ -14,7 +14,7 @@
 MESH = pl.DeviceIdType.MESH
 f32 = jnp.float32
 bf16 = jnp.bfloat16
-N_SEM = 64
+N_SEM = 53
 BLK = (8, 2, 4, 2, 32, 128)
 
 
@@ -102,7 +102,7 @@
     tok, w0, w1, w2, o0, o1, o2, acc, qkv, cotb, scores, mixl, d_loc, dmix, d_all, d_oth, att_oth, att_snd,
     st_snd, st_rcv, bk_snd, bk_rcv, prior, later,
     p0, p1, p2, sa, ra, acc_a, acc_b, acc_c,
-    sa_y, ra_y, sa_x, ra_x, acc_a2, sb_y, rb_y, sb_z, rb_z, acc_b2, sc_x, rc_x, sc_z, rc_z, acc_c2,
+    sa_x, ra_x, sb_y, rb_y, sb_z, rb_z, acc_b2, sc_x, rc_x, sc_z, rc_z, acc_c2,
     sb_d, rb_d, sc_d, rc_d, sizes, send_sems, recv_sems, loc_sems,
 ):
     rep, seq = lax.axis_index("rep"), lax.axis_index("seq")
@@ -144,9 +144,9 @@
     def cols(p):
         return pl.ds(pl.multiple_of(mod(z + OFF[p], 8) * 512, 512), 512)
 
-    peers = [partner] + [xd(k) for k in (1, 2, 3)] + [yd(k) for k in (1, 2, 3)] + [zd(k) for k in range(1, 8)]
-    peers += [gd(dx, 1) for dx in (1, 2, 3)]
-    peers += [dev(mod(x + k, 4), y, z, oc) for k in (1, 2, 3)] + [dev(x, y, mod(z + k, 8), oc) for k in range(1, 8)]
+    plane = [(dx, dy) for dx in (2, 1, 3, 0) for dy in (2, 1, 3, 0) if dx or dy]
+    peers = [partner] + [dev(x, y, mod(z + k, 8), c_) for k in (4, 3, 5, 2, 6, 1, 7) for c_ in (c, oc)]
+    peers += [dev(mod(x + dx, 4), mod(y + dy, 4), z, c_) for dx, dy in plane for c_ in (c, oc)]
     bar = pltpu.get_barrier_semaphore()
     for to in peers:
         pl.semaphore_signal(bar, inc=1, device_id=to, device_id_type=MESH)
@@ -382,6 +382,7 @@
             later[0] += got
             later[1] += got
 
+    r2 = a_out(2, ends, r1)
     for b, r in enumerate(rows):
         l_hi, l_lo = split(later[b])
         k, v = qkv[r, 128:256], qkv[r, 256:384]
@@ -436,15 +437,14 @@
             d = jnp.concatenate([d_all[mine, :], d_oth[...]], 1)
             gt_o[:, cols(p)] = dot(d, w, 1, 1).astype(bf16)
 
-    r2 = a_out(2, ends, r1)
     p_kv(ge)
     d_e = direct(ge)
     p_qkv(gc)
     d_c = direct(gc)
     r3f = a_out(3, free, r2f)
-    r3 = a_out(3, ends, r2)
     p_qkv(gb)
     d_b = direct(gb)
+    r3 = a_out(3, ends, r2)
     p_qkv(ga)
     d_a = direct(ga)
     d_x.wait()
@@ -458,36 +458,31 @@
     t_c = third(gc, d_c)
     g_t(3)
     t_b = third(gb, d_b)
+    t_a = third(ga, d_a)
     r4f.wait()
     r4.wait()
-    acc_a[...] = p0[0] + ra[0, 3].astype(f32) + ra[1, 3].astype(f32)
-    a_y2 = Batch(net)
-    for k in (2, 1, 3):
-        at = mod(y + k, 4)
-        sa_y[k - 1] = acc_a[lax.div(at, jnp.int32(2)), :, mod(at, 2)].astype(bf16)
-        a_y2.send(sa_y.at[k - 1], ra_y.at[k - 1], yd(k))
-    t_a = third(ga, d_a)
+    acc_a[...] = (p0[0] + ra[0, 3].astype(f32) + ra[1, 3].astype(f32)).reshape(2, 4, 2, 2, 16, HD)
+    sa_x[...] = acc_a[...].astype(bf16)
+    for i, (dx, dy) in enumerate(plane):
+        ax, ay = mod(x + dx, 4), mod(y + dy, 4)
+        part = sa_x.at[lax.div(ay, jnp.int32(2)), ax, mod(ay, 2)]
+        last.send(part.at[c], ra_x.at[0, i], dev(ax, ay, z, c))
+        last.send(part.at[oc], ra_x.at[1, i], dev(ax, ay, z, oc))
+    last.send(sa_x.at[yh, x, yl, oc], ra_x.at[1, 15], partner)
     fourth(ge, t_e)
+    fourth(gc, t_c)
     g_t(4)
-    fourth(gc, t_c)
     fourth(gb, t_b)
-    a_y2.wait()
-    acc_a2[...] = (acc_a[yh, :, yl] + sum(ra_y[k].astype(f32) for k in range(3))).reshape(4, 2, 16, HD)
-    sa_x[...] = acc_a2[...].astype(bf16)
-    last.send(sa_x.at[x, oc], ra_x.at[1, 0], partner)
-    for k in (2, 1, 3):
-        at = mod(x + k, 4)
-        last.send(sa_x.at[at, c], ra_x.at[0, k], xd(k))
-        last.send(sa_x.at[at, oc], ra_x.at[1, k], dev(at, y, z, oc))
+    g_t(5)
     fourth(ga, t_a)
-    g_t(5, 6, 7)
+    g_t(6, 7)
     att_o[:, lane_c] = att_snd[c]
     att_x.wait()
     att_o[:, lane_o] = att_oth[...]
     scale = 1.0 / T_DEV
     last.wait()
-    gq_o[:, lane_c] = (acc_a2[x, c] + sum(ra_x[0, k].astype(f32) for k in range(1, 4))) * scale
-    gq_o[:, lane_o] = sum(ra_x[1, k].astype(f32) for k in range(4)) * scale
+    gq_o[:, lane_c] = (acc_a[yh, x, yl, c] + sum(ra_x[0, k].astype(f32) for k in range(15))) * scale
+    gq_o[:, lane_o] = sum(ra_x[1, k].astype(f32) for k in range(16)) * scale
     for out, total, rcv in ((gk_o, acc_b2, rb_z), (gv_o, acc_c2, rc_z)):
         out[:, lane_c] = (total[0, c] + sum(rcv[0, p].astype(f32) for p in range(1, 8))) * scale
         out[:, lane_o] = sum(rcv[1, p].astype(f32) for p in range(8)) * scale
@@ -516,8 +511,8 @@
     scratch += [v(128, 128), v(7, 128, 128), v(128, 128), v(7, 128, 128), v(2, 128, 128, t=f32), v(2, 128, 128, t=f32)]
     scratch += [v(*BLK, t=f32)] * 3
     scratch += [v(2, 4, 2, 4, 2, 32, 128)] * 2
-    scratch += [v(2, 4, 2, 32, 128, t=f32), v(8, 2, 2, 32, 128, t=f32), v(8, 4, 32, 128, t=f32)]
-    scratch += [v(3, 4, 32, 128)] * 2 + [v(4, 2, 16, 128), v(2, 4, 16, 128)] + [v(4, 2, 16, 128, t=f32)]
+    scratch += [v(2, 4, 2, 2, 16, 128, t=f32), v(8, 2, 2, 32, 128, t=f32), v(8, 4, 32, 128, t=f32)]
+    scratch += [v(2, 4, 2, 2, 16, 128), v(2, 16, 16, 128)]
     scratch += [v(3, 8, 32, 128)] * 2 + [v(8, 2, 16, 128), v(2, 8, 16, 128)] + [v(8, 2, 16, 128, t=f32)]
     scratch += [v(3, 8, 32, 128)] * 2 + [v(8, 2, 16, 128), v(2, 8, 16, 128)] + [v(8, 2, 16, 128, t=f32)]
     scratch += [v(3, 8, 2, 2, 32, 128)] * 2 + [v(3, 8, 4, 32, 128)] * 2 + [v(160, 16, 128)]

time: 68.2 us -> 67.5 us (0.990)
  Pallas kernels: 67.3 us -> 66.6 us
    pallas_call x1, Pallas kernels: 65.2 us -> 64.4 us  [body(): pl.pallas_call(kernel, out_shape=(pltpu.VMEM((T_DEV, 256), bf16), pltpu.V...]
where the time goes in v4:
time: 67.5 us; the launch traced here: 67.4 us
  Pallas kernels  66.6 us (99%)
  between operations  0.8 us (1%)
    pallas_call x1, Pallas kernels, body(): pl.pallas_call(kernel, out_shape=(pltpu.VMEM((T_DEV, 256), bf16), pltpu.V...  64.4 us
    pallas_call x1, Pallas kernels, body(): pl.pallas_call(write_out, out_shape=[jax.ShapeDtypeStruct(o.shape, o.dtyp...  2.14 us

profile of v4, /device:TPU:1, one launch (start us, length us, event | category | flops | bytes accessed | tf_op | source)
XLA Modules:
  0.0 67.4 jit_solution(12728726973485376398)
XLA Ops:
  0.6 64.4 %step.1 = (bf16[512,256]{1,0:T(8,128)(2,1)S(1)}, bf16[512,4096]{1,0:T(8,128)(2,1)S(1)}, f32[16,256]{1,0:T(8,128)S(1)}, f32[16,256]{1,0:T(8,128)S(1)}, f32[16,256]{1,0:T(8,128)S(1)}) custom-call(bf16[512,4096]{1,0:T(8,128)(2,1)} %tok_hbm.1, bf16[4,2,32,256]{3,2,1,0:T(8,128)(2,1)} %bitcast.3, bf16[4,2,32,256]{3,2,1,0:T(8,128)(2,1)} %bitcast.4, ...), custom_call_target="tpu_custom_call" | custom-call | flops 10000000000 | bytes 10000000 | tf_op jit(solution)/shard_map/step/pallas_call | solution.py:522
  65.1 2.1 %write_out.1 = (bf16[512,256]{1,0:T(8,128)(2,1)}, bf16[512,4096]{1,0:T(8,128)(2,1)}, f32[16,256]{1,0:T(8,128)}, f32[16,256]{1,0:T(8,128)}, f32[16,256]{1,0:T(8,128)}) custom-call(bf16[512,256]{1,0:T(8,128)(2,1)S(1)} %get-tuple-element.10.refs_0_, bf16[512,4096]{1,0:T(8,128)(2,1)S(1)} %get-tuple-element.11.refs_1_, f32[16,256]{1,0:T(8,128)S(1)} %get-tuple-element.12.refs_2_, ...), custom_call_target="tpu_custom_call" | custom-call | tf_op jit(solution)/shard_map/write_out/pallas_call | solution.py:538

commit v5 on v4

--- a/solution.py
+++ b/solution.py
@@ -125,7 +125,7 @@
 
     partner = dev(x, y, z, oc)
     across = dev(x, 3 - y, z, c)
-    group = [(dx, dl) for dx in range(4) for dl in range(2) if dx or dl]
+    group = [(dx, dl) for dx in (2, 1, 3, 0) for dl in (1, 0) if dx or dl]
 
     def gd(dx, dl):
         return dev(mod(x + dx, 4), yh * 2 + mod(yl + dl, 2), z, c)
@@ -225,10 +225,10 @@
     cot_x = net.one(cot.at[:, lane_o], cotb.at[c], partner)
     tok_x = net.one(tok_hbm, tok.at[mine], partner)
 
+    rows = [slice(0, 512), slice(512, 1024)]
+
     def project(ps, lanes, ws, first):
-        @pl.loop(0, 2)
-        def _(i):
-            r = pl.ds(pl.multiple_of(i * 512, 512), 512)
+        for r in rows:
             got = None
             for p in ps:
                 w = jnp.concatenate([w[p].reshape(512, HD) for w in ws], 1)
@@ -276,7 +276,6 @@
     w_x = [net.one(w1, o1, partner), net.one(w2, o2, partner)]
     kv_acc(ge)
 
-    rows = [slice(0, 512), slice(512, 1024)]
     state = []
     for r in rows:
         qkv[r, 128:384] = acc[r, 128:384].astype(bf16)
@@ -372,6 +371,8 @@
     p_q(5)
     p_q(6)
     r2f = a_out(2, free)
+    p_q(3)
+    p_q(4)
 
     for i, (dx, dl) in enumerate(group):
 
@@ -439,7 +440,7 @@
 
     p_kv(ge)
     d_e = direct(ge)
-    p_qkv(gc)
+    p_kv(gc)
     d_c = direct(gc)
     r3f = a_out(3, free, r2f)
     p_qkv(gb)

time: 67.5 us -> 66.6 us (0.987)
  Pallas kernels: 66.6 us -> 65.7 us
    pallas_call x1, Pallas kernels: 64.4 us -> 63.5 us  [body(): pl.pallas_call(kernel, out_shape=(pltpu.VMEM((T_DEV, 256), bf16), pltpu.V...]
where the time goes in v5:
time: 66.6 us; the launch traced here: 66.5 us
  Pallas kernels  65.7 us (99%)
  between operations  0.8 us (1%)
    pallas_call x1, Pallas kernels, body(): pl.pallas_call(kernel, out_shape=(pltpu.VMEM((T_DEV, 256), bf16), pltpu.V...  63.5 us
    pallas_call x1, Pallas kernels, body(): pl.pallas_call(write_out, out_shape=[jax.ShapeDtypeStruct(o.shape, o.dtyp...  2.14 us

profile of v5, /device:TPU:1, one launch (start us, length us, event | category | flops | bytes accessed | tf_op | source)
XLA Modules:
  0.0 66.5 jit_solution(14665308593554516903)
XLA Ops:
  0.6 63.5 %step.1 = (bf16[512,256]{1,0:T(8,128)(2,1)S(1)}, bf16[512,4096]{1,0:T(8,128)(2,1)S(1)}, f32[16,256]{1,0:T(8,128)S(1)}, f32[16,256]{1,0:T(8,128)S(1)}, f32[16,256]{1,0:T(8,128)S(1)}) custom-call(bf16[512,4096]{1,0:T(8,128)(2,1)} %tok_hbm.1, bf16[4,2,32,256]{3,2,1,0:T(8,128)(2,1)} %bitcast.3, bf16[4,2,32,256]{3,2,1,0:T(8,128)(2,1)} %bitcast.4, ...), custom_call_target="tpu_custom_call" | custom-call | flops 10000000000 | bytes 10000000 | tf_op jit(solution)/shard_map/step/pallas_call | solution.py:523
  64.2 2.1 %write_out.1 = (bf16[512,256]{1,0:T(8,128)(2,1)}, bf16[512,4096]{1,0:T(8,128)(2,1)}, f32[16,256]{1,0:T(8,128)}, f32[16,256]{1,0:T(8,128)}, f32[16,256]{1,0:T(8,128)}) custom-call(bf16[512,256]{1,0:T(8,128)(2,1)S(1)} %get-tuple-element.10.refs_0_, bf16[512,4096]{1,0:T(8,128)(2,1)S(1)} %get-tuple-element.11.refs_1_, f32[16,256]{1,0:T(8,128)S(1)} %get-tuple-element.12.refs_2_, ...), custom_call_target="tpu_custom_call" | custom-call | tf_op jit(solution)/shard_map/write_out/pallas_call | solution.py:539

commit v6 on v5

--- a/solution.py
+++ b/solution.py
@@ -454,8 +454,9 @@
     g_t(0)
     r4f = a_out(4, free, r3f)
     r4 = a_out(4, ends, r3)
-    g_t(1, 2)
+    g_t(1)
     t_e = third(ge, d_e)
+    g_t(2)
     t_c = third(gc, d_c)
     g_t(3)
     t_b = third(gb, d_b)

time: 66.6 us -> 66.6 us (level)
  no operation moved by 1% of the time
where the time goes in v6:
time: 66.6 us; the launch traced here: 66.5 us
  Pallas kernels  65.7 us (99%)
  between operations  0.8 us (1%)
    pallas_call x1, Pallas kernels, body(): pl.pallas_call(kernel, out_shape=(pltpu.VMEM((T_DEV, 256), bf16), pltpu.V...  63.5 us
    pallas_call x1, Pallas kernels, body(): pl.pallas_call(write_out, out_shape=[jax.ShapeDtypeStruct(o.shape, o.dtyp...  2.14 us

profile of v6, /device:TPU:1, one launch (start us, length us, event | category | flops | bytes accessed | tf_op | source)
XLA Modules:
  0.0 66.5 jit_solution(9093628391176344420)
XLA Ops:
  0.6 63.5 %step.1 = (bf16[512,256]{1,0:T(8,128)(2,1)S(1)}, bf16[512,4096]{1,0:T(8,128)(2,1)S(1)}, f32[16,256]{1,0:T(8,128)S(1)}, f32[16,256]{1,0:T(8,128)S(1)}, f32[16,256]{1,0:T(8,128)S(1)}) custom-call(bf16[512,4096]{1,0:T(8,128)(2,1)} %tok_hbm.1, bf16[4,2,32,256]{3,2,1,0:T(8,128)(2,1)} %bitcast.3, bf16[4,2,32,256]{3,2,1,0:T(8,128)(2,1)} %bitcast.4, ...), custom_call_target="tpu_custom_call" | custom-call | flops 10000000000 | bytes 10000000 | tf_op jit(solution)/shard_map/step/pallas_call | solution.py:524
  64.2 2.1 %write_out.1 = (bf16[512,256]{1,0:T(8,128)(2,1)}, bf16[512,4096]{1,0:T(8,128)(2,1)}, f32[16,256]{1,0:T(8,128)}, f32[16,256]{1,0:T(8,128)}, f32[16,256]{1,0:T(8,128)}) custom-call(bf16[512,256]{1,0:T(8,128)(2,1)S(1)} %get-tuple-element.10.refs_0_, bf16[512,4096]{1,0:T(8,128)(2,1)S(1)} %get-tuple-element.11.refs_1_, f32[16,256]{1,0:T(8,128)S(1)} %get-tuple-element.12.refs_2_, ...), custom_call_target="tpu_custom_call" | custom-call | tf_op jit(solution)/shard_map/write_out/pallas_call | solution.py:540
